TPU v7x, 512 devices: a whole 4x8x8 slice. The times are simulated.
512 devices in a mesh: user: 32 (over z, x), tensor: 16 (over y, core).
Axes of the slice: x: 4, y: 8, z: 8, core: 2. Of those that a mesh axis runs over, the one named last changes fastest.
Arguments:
- activations: bfloat16 [2, 24576, 8192], P(None, 'user', 'tensor'), may hold values from -70 to 70, as said below
- key_grads: bfloat16 [2, 24576, 1024], P(None, 'user'), may hold values from -2.4 to 2.4
- row_users: int32 [2, 24576], P(None, 'user'), may hold values from 0 to 7, as said below
Outputs:
- clipped_mean: float32 [1024, 8192], P('user', 'tensor')
Inputs may be any that keep to these rules, and one draw needn't show every extreme that they name: `activations`: activations are finite. `row_users`: every aligned block of 768 rows names every user 0 to 7 at least once.
All inputs are finite; a program needn't handle non-finite values.
Results may differ from a plain program's by a relative error of at most 0.0012.
Values sent between devices are 32-bit elements; how exact they have to be, the bound alone decides.
No kernel may reach another device: no remote copies, remote signals or barrier semaphores. Data moves between devices by JAX's collectives and lax.ppermute only.
A program may use at most 64 MiB of HBM per device.

v0:
```python
import math

import jax
import jax.numpy as jnp
from jax import lax
from jax.sharding import PartitionSpec as P

D = 8192
KV = 1024
ROWS = 768
USERS_MB = 8


def user_table(owners):
    labels = lax.broadcasted_iota(jnp.int32, (USERS_MB, owners.shape[0]), 0)
    return (owners[None, :] == labels).astype(jnp.float32)


def local_norms(inputs, gradient, owners):
    xgram = jnp.dot(inputs, inputs.T, preferred_element_type=jnp.float32)
    ggram = jnp.dot(gradient, gradient.T, preferred_element_type=jnp.float32)
    table = user_table(owners)
    spread = jnp.dot(table, xgram * ggram, precision=lax.Precision.HIGHEST)
    return jnp.sum(spread * table, axis=1)


def clip_rows(gradient, owners, squares, bound):
    factor = bound / jnp.maximum(jnp.sqrt(squares), bound)
    row_factor = jnp.sum(user_table(owners) * factor[:, None], axis=0)
    return (gradient.astype(jnp.float32) * row_factor[:, None]).astype(jnp.bfloat16)


def grad_rows(weighted, inputs):
    return lax.dot_general(
        weighted, inputs, (((0,), (0,)), ((), ())), preferred_element_type=jnp.float32
    )


def joined_rows(weighted_list, input_list):
    total = grad_rows(weighted_list[0], input_list[0])
    total = total + grad_rows(weighted_list[1], input_list[1])
    return total


def body(activations, key_grads, row_users):
    batches = activations.shape[0]
    bound = 0.3 * math.sqrt(D * KV * ROWS / USERS_MB)
    squares = [
        lax.psum(
            local_norms(activations[micro_index], key_grads[micro_index], row_users[micro_index]),
            "tensor",
        )
        for micro_index in range(batches)
    ]
    weighted = [
        clip_rows(key_grads[micro_index], row_users[micro_index], squares[micro_index], bound)
        for micro_index in range(batches)
    ]
    input_list = [activations[micro_index] for micro_index in range(batches)]
    total = lax.psum_scatter(
        joined_rows(weighted, input_list), "user", scatter_dimension=0, tiled=True
    )
    return total / (batches * lax.axis_size("user") * USERS_MB)


def solution(mesh):
    return jax.shard_map(
        body,
        mesh=mesh,
        in_specs=(P(None, "user", "tensor"), P(None, "user", None), P(None, "user")),
        out_specs=P("user", "tensor"),
        check_vma=False,
    )
```

profile of v0, /device:TPU:6, one launch (start us, length us, event | category | flops | bytes accessed | tf_op | source)
XLA Modules:
  0.0 278.4 jit_solution(12494304357999799829)
XLA Ops:
  6.5 0.0 copy-start.1
  6.5 0.0 reduce-scatter.2.cloned.1.call-start
  6.5 3.5 %fusion.9 = f32[768,768]{1,0:T(8,128)S(1)} fusion(bf16[2,768,1024]{2,1,0:T(8,128)(2,1)} %param.4), kind=kOutput, calls=%fused_computation.10 | convolution fusion | flops 1207959552 | bytes 3932160 | tf_op jit(solution)/shard_map/dot_general | solution.py:21
  10.0 0.0 copy-done.1
  10.0 0.0 copy-start.2
  10.1 1.4 fusion.11
  11.5 0.0 copy-done.2
  11.5 0.8 fusion.32
  12.3 0.0 copy-start
  12.3 0.8 fusion.35
  13.1 0.0 copy-done
  13.2 1.1 fusion.25
  14.2 1.1 fusion.28
  15.3 26.4 %all-reduce = (f32[8]{0:T(128)S(1)}, f32[8]{0:T(128)S(1)}) all-reduce(f32[8]{0:T(128)S(1)} %fusion.28, f32[8]{0:T(128)S(1)} %fusion.25), channel_id=1, replica_groups=mesh['user'=32,'tensor'=16] {'tensor'}, use_global_device_ids=true, to_apply=%region_1.0 | all-reduce | flops 16 | bytes 128 | tf_op jit(solution)/shard_map/psum | solution.py:49
  41.8 0.1 select_reduce_fusion
  41.9 0.0 copy-start.3
  41.9 2.4 fusion.5
  44.3 0.0 copy-done.3
  44.3 2.5 convolution_add_fusion
  46.8 0.0 reduce-scatter.2.cloned.1.call-update
  46.8 223.3 %reduce-scatter.2.cloned.1.call-done = f32[32,512]{1,0:T(8,128)} async-done(((f32[1024,512]{1,0:T(8,128)}), f32[32,512]{1,0:T(8,128)}) %reduce-scatter.2.cloned.1.call-update) | async-done | bytes 65552 | tf_op jit(solution)/shard_map/reduce_scatter | solution.py:60
  270.1 1.5 broadcast_multiply_fusion
  (3 shorter events, 0.0 us)
Async XLA Ops:
  6.5 3.5 %copy-start.1 = (bf16[2,768,1024]{2,1,0:T(8,128)(2,1)S(1)}, bf16[2,768,1024]{2,1,0:T(8,128)(2,1)}, u32[]{:S(2)}) copy-start(bf16[2,768,1024]{2,1,0:T(8,128)(2,1)} %param.4) | copy-start | bytes 9437188
  6.5 263.6 %reduce-scatter.2.cloned.1.call-start = ((), (), s32[]{:S(2)}) async-start(), calls=%async_computation.1 | async-start | bytes 2162688 | tf_op jit(solution)/shard_map/reduce_scatter | solution.py:60
  10.0 1.4 copy-start.2
  12.3 0.8 copy-start
  41.9 2.4 copy-start.3
Sparse Core Ops, SparseCore 0:
  46.9 223.1 reduce-scatter.1
where the time goes:
time: 279 us; the launch traced here: 278 us
  waiting for transfers between devices  223 us (80%)
  blocking collectives  26.4 us (9%)
  matrix products  13.5 us (5%)
  between operations  13.5 us (5%)
    reduce_scatter x1, waiting for transfers between devices, body(): lax.psum_scatter(joined_rows(weighted, input_list), 'user', scatter_dimen...  223 us
    psum x1, blocking collectives, body(): lax.psum(local_norms(activations[micro_index], key_grads[micro_index], ro...  26.4 us
  transfers between devices with their start and end apart: 1, of which 1 were waited for; matrix products, arithmetic and copies ran while one was open for 0% of the time, Pallas kernels for 0%

commit v1 on v0

v1 whole, which is shorter than its diff:
```python
import math

import jax
import jax.numpy as jnp
from jax import lax
from jax.sharding import Mesh, PartitionSpec as P

D = 8192
KV = 1024
ROWS = 768
USERS_MB = 8
NZ, NX, NY, NC = 8, 4, 8, 2


def user_table(owners):
    labels = lax.broadcasted_iota(jnp.int32, (USERS_MB, owners.shape[0]), 0)
    return (owners[None, :] == labels).astype(jnp.float32)


def local_norms(inputs, gradient, owners):
    xgram = jnp.dot(inputs, inputs.T, preferred_element_type=jnp.float32)
    ggram = jnp.dot(gradient, gradient.T, preferred_element_type=jnp.float32)
    table = user_table(owners)
    spread = jnp.dot(table, xgram * ggram, precision=lax.Precision.HIGHEST)
    return jnp.sum(spread * table, axis=1)


def clip_rows(gradient, owners, squares, bound):
    factor = bound / jnp.maximum(jnp.sqrt(squares), bound)
    row_factor = jnp.sum(user_table(owners) * factor[:, None], axis=0)
    return (gradient.astype(jnp.float32) * row_factor[:, None]).astype(jnp.bfloat16)


def body(activations, key_grads, row_users):
    batches = activations.shape[0]
    bound = 0.3 * math.sqrt(D * KV * ROWS / USERS_MB)
    partial = jnp.stack([
        local_norms(activations[m], key_grads[m], row_users[m]) for m in range(batches)
    ])
    shared = NY * NC
    spread = jnp.broadcast_to(partial[None], (shared,) + partial.shape)
    squares = jnp.sum(lax.all_to_all(spread, ("y", "core"), 0, 0), axis=0)
    weighted = jnp.stack([
        clip_rows(key_grads[m], row_users[m], squares[m], bound) for m in range(batches)
    ])
    total = lax.dot_general(
        weighted.reshape(batches * ROWS, KV),
        activations.reshape(batches * ROWS, -1),
        (((0,), (0,)), ((), ())),
        preferred_element_type=jnp.float32,
    ) * (1.0 / (batches * NZ * NX * USERS_MB))
    width = total.shape[1]
    rows = KV // (NZ * NX)
    total = total.reshape(NZ, NX, rows, width).swapaxes(0, 1)
    total = jnp.sum(lax.all_to_all(total, "x", 0, 0), axis=0)
    return jnp.sum(lax.all_to_all(total, "z", 0, 0), axis=0)


def solution(mesh):
    split = Mesh(mesh.devices.reshape(NZ, NX, NY, NC), ("z", "x", "y", "core"))
    user, tensor = ("z", "x"), ("y", "core")
    return jax.shard_map(
        body,
        mesh=split,
        in_specs=(P(None, user, tensor), P(None, user, None), P(None, user)),
        out_specs=P(user, tensor),
        check_vma=False,
    )
```

time: 279 us -> 85.6 us (0.31)
  waiting for transfers between devices: 223 us -> 1.86 us
  blocking collectives: 26.4 us -> 55.6 us
  between operations: 13.5 us -> 0.15 us
  local copies, waits for them, and re-layouts: 0.05 us -> 7.78 us
  starting transfers between devices: 0.01 us -> 7.2 us
  matrix products: 13.5 us -> 10.4 us
    reduce_scatter x1 -> x0, waiting for transfers between devices: 223 us -> none  [body(): lax.psum_scatter(joined_rows(weighted, input_list), 'user', scatter_dimen...]
    all_to_all x0 -> x2, blocking collectives: none -> 55.6 us  [the longest x1 29.4 us: body(): total = jnp.sum(lax.all_to_all(total, 'x', 0, 0), axis=0)]
    psum x1 -> x0, blocking collectives: 26.4 us -> none  [body(): lax.psum(local_norms(activations[micro_index], key_grads[micro_index], ro...]
    all_to_all x0 -> x1, starting transfers between devices: none -> 7.2 us  [body(): squares = jnp.sum(lax.all_to_all(spread, ('y', 'core'), 0, 0), axis=0)]
    unnamed x8 -> x10, local copies, waits for them, and re-layouts: 0.02 us -> 3.53 us
    slice x1 -> x2, local copies, waits for them, and re-layouts: 0.02 us -> 3.36 us  [the longest x1 3.34 us: body(): key_grads[m]]
    dot_general x2 -> x1, matrix products: 4.84 us -> 1.78 us  [body(): lax.dot_general(weighted.reshape(batches * ROWS, KV), activations.reshape...]
  transfers between devices with their start and end apart: 1 -> 1, of which waited for: 1 -> 1; matrix products, arithmetic and copies ran while one was open for 0% -> 7% of each run, Pallas kernels for 0% -> 0%
where the time goes in v1:
time: 85.6 us; the launch traced here: 84.6 us
  blocking collectives  55.6 us (65%)
  matrix products  10.4 us (12%)
  local copies, waits for them, and re-layouts  7.78 us (9%)
  starting transfers between devices  7.2 us (8%)
  waiting for transfers between devices  1.86 us (2%)
  other arithmetic  1.63 us (2%)
    all_to_all x1, blocking collectives, body(): total = jnp.sum(lax.all_to_all(total, 'x', 0, 0), axis=0)  29.4 us
    all_to_all x1, blocking collectives, body(): return jnp.sum(lax.all_to_all(total, 'z', 0, 0), axis=0)  26.2 us
    all_to_all x1, starting transfers between devices, body(): squares = jnp.sum(lax.all_to_all(spread, ('y', 'core'), 0, 0), axis=0)  7.2 us
    dot_general x2, matrix products, local_norms(): ggram = jnp.dot(gradient, gradient.T, preferred_element_type=jnp.float32)  4.87 us
    unnamed x10, local copies, waits for them, and re-layouts  3.53 us
    slice x1, local copies, waits for them, and re-layouts, body(): key_grads[m]  3.34 us
    dot_general x2, matrix products, local_norms(): spread = jnp.dot(table, xgram * ggram, precision=lax.Precision.HIGHEST)  2.16 us
    all_to_all x1, waiting for transfers between devices, body(): squares = jnp.sum(lax.all_to_all(spread, ('y', 'core'), 0, 0), axis=0)  1.86 us
  transfers between devices with their start and end apart: 1, of which 1 were waited for; matrix products, arithmetic and copies ran while one was open for 7% of the time, Pallas kernels for 0%

profile of v1, /device:TPU:6, one launch (start us, length us, event | category | flops | bytes accessed | tf_op | source)
XLA Modules:
  0.0 84.6 jit_solution(5945999720696284071)
XLA Ops:
  0.0 0.0 copy-start
  0.0 3.5 %fusion.12 = f32[768,768]{1,0:T(8,128)S(1)} fusion(bf16[2,768,1024]{2,1,0:T(8,128)(2,1)} %param.4), kind=kOutput, calls=%fused_computation.14 | convolution fusion | flops 1207959552 | bytes 3932160 | tf_op jit(solution)/shard_map/dot_general | solution.py:22
  3.5 0.0 copy-done
  3.5 0.0 copy-start.2
  3.5 1.4 %fusion.10 = f32[768,768]{1,0:T(8,128)S(1)} fusion(bf16[2,768,1024]{2,1,0:T(8,128)(2,1)S(1)} %copy-done), kind=kOutput, calls=%fused_computation.12 | convolution fusion | flops 1207959552 | bytes 3932160 | tf_op jit(solution)/shard_map/dot_general | solution.py:22
  4.9 0.0 copy-done.2
  4.9 0.8 fusion.28
  5.7 0.0 copy-start.1
  5.7 0.8 fusion.26
  6.6 0.0 copy-done.1
  6.6 1.1 %fusion.23 = f32[8]{0:T(128)S(1)} fusion(f32[768,768]{1,0:T(8,128)S(1)} %fusion.28, f32[768,768]{1,0:T(8,128)S(1)} %fusion.12, s32[768]{0:T(1024)S(1)} %get-tuple-element.5), kind=kOutput, calls=%fused_computation.19 | convolution fusion | flops 57237496 | bytes 4721696 | tf_op jit(solution)/shard_map/dot_general | solution.py:24
  7.7 1.1 %fusion.20 = f32[8]{0:T(128)S(1)} fusion(f32[768,768]{1,0:T(8,128)S(1)} %fusion.26, f32[768,768]{1,0:T(8,128)S(1)} %fusion.10, s32[768]{0:T(1024)S(1)} %get-tuple-element.6), kind=kOutput, calls=%fused_computation.18 | convolution fusion | flops 57237496 | bytes 4721696 | tf_op jit(solution)/shard_map/dot_general | solution.py:24
  8.8 0.6 broadcast_in_dim.2
  9.4 7.2 %all-to-all-start = ((f32[16,2,8]{2,1,0:T(2,128)}), f32[16,2,8]{2,1,0:T(2,128)S(1)}, u32[]{:S(2)}, u32[]{:S(2)}) async-start(f32[16,2,8]{2,1,0:T(2,128)} %broadcast_in_dim.2), calls=%async_computation | async-start | bytes 32768 | tf_op jit(solution)/shard_map/all_to_all | solution.py:42
  16.6 3.3 %fusion.37 = (bf16[1,768,1024]{2,1,0:T(8,128)(2,1)S(1)}, bf16[1,768,1024]{2,1,0:T(8,128)(2,1)}) fusion(bf16[2,768,1024]{2,1,0:T(8,128)(2,1)} %param.4), kind=kLoop, calls=%fused_computation.40 | loop fusion | bytes 6291456 | tf_op jit(solution)/shard_map/slice | solution.py:44
  19.9 0.7 copy.17
  20.6 1.7 %copy.18 = bf16[1,768,1024]{1,2,0:T(8,128)(2,1)S(1)} copy(bf16[1,768,1024]{2,1,0:T(8,128)(2,1)} %get-tuple-element.8) | data formatting | bytes 3145728
  22.4 1.9 %all-to-all-done = f32[16,2,8]{2,1,0:T(2,128)S(1)} async-done(((f32[16,2,8]{2,1,0:T(2,128)}), f32[16,2,8]{2,1,0:T(2,128)S(1)}, u32[]{:S(2)}, u32[]{:S(2)}) %all-to-all-start) | async-done | bytes 1056 | tf_op jit(solution)/shard_map/all_to_all | solution.py:42
  24.3 0.1 select_reduce_fusion
  24.4 0.3 multiply_convert_fusion.1
  24.7 0.0 copy-start.3
  24.7 0.3 multiply_convert_fusion
  25.0 1.1 %copy-done.3 = bf16[2,768,512]{2,1,0:T(8,128)(2,1)S(1)} copy-done((bf16[2,768,512]{2,1,0:T(8,128)(2,1)S(1)}, bf16[2,768,512]{2,1,0:T(8,128)(2,1)}, u32[]{:S(2)}) %copy-start.3) | copy-done | bytes 1572888
  26.1 1.8 %bitcast_multiply_fusion = f32[1024,512]{1,0:T(8,128)S(1)} fusion(bf16[2,768,512]{2,1,0:T(8,128)(2,1)S(1)} %copy-done.3, bf16[1,768,1024]{1,2,0:T(8,128)(2,1)S(1)} %multiply_convert_fusion, bf16[1,768,1024]{1,2,0:T(8,128)(2,1)S(1)} %multiply_convert_fusion.1), kind=kOutput, calls=%fused_computation.10 | convolution fusion | flops 1612709888 | bytes 6815744 | tf_op jit(solution)/shard_map/dot_general | solution.py:46
  27.9 0.3 copy.22
  28.2 29.4 %all_to_all.15 = f32[4,8,32,512]{3,2,1,0:T(8,128)S(1)} all-to-all(f32[4,8,32,512]{3,2,1,0:T(8,128)S(1)} %bitcast.29), channel_id=1, replica_groups=mesh['z'=8,'x'=4,'y'=8,'core'=2] {'x'}, dimensions={0} | all-to-all | bytes 4194304 | tf_op jit(solution)/shard_map/all_to_all | solution.py:55
  57.5 0.2 reduce_sum.68
  57.8 26.2 %all_to_all.16 = f32[8,32,512]{2,1,0:T(8,128)S(1)} all-to-all(f32[8,32,512]{2,1,0:T(8,128)S(1)} %reduce_sum.68), channel_id=1, replica_groups=mesh['z'=8,'x'=4,'y'=8,'core'=2] {'z'}, dimensions={0} | all-to-all | bytes 1048576 | tf_op jit(solution)/shard_map/all_to_all | solution.py:56
  83.9 0.7 reduce_sum.69
  (4 shorter events, 0.1 us)
Async XLA Ops:
  0.0 3.5 %copy-start = (bf16[2,768,1024]{2,1,0:T(8,128)(2,1)S(1)}, bf16[2,768,1024]{2,1,0:T(8,128)(2,1)}, u32[]{:S(2)}) copy-start(bf16[2,768,1024]{2,1,0:T(8,128)(2,1)} %param.4) | copy-start | bytes 9437188
  3.5 1.4 %copy-start.2 = (bf16[2,768,512]{2,1,0:T(8,128)(2,1)S(1)}, bf16[2,768,512]{2,1,0:T(8,128)(2,1)}, u32[]{:S(2)}) copy-start(bf16[2,768,512]{2,1,0:T(8,128)(2,1)} %param.3) | copy-start | bytes 4718596
  5.7 0.8 copy-start.1
  9.4 14.8 %all-to-all-start = ((f32[16,2,8]{2,1,0:T(2,128)}), f32[16,2,8]{2,1,0:T(2,128)S(1)}, u32[]{:S(2)}, u32[]{:S(2)}) async-start(f32[16,2,8]{2,1,0:T(2,128)} %broadcast_in_dim.2), calls=%async_computation | async-start | bytes 32768 | tf_op jit(solution)/shard_map/all_to_all | solution.py:42
  24.7 1.4 %copy-start.3 = (bf16[2,768,512]{2,1,0:T(8,128)(2,1)S(1)}, bf16[2,768,512]{2,1,0:T(8,128)(2,1)}, u32[]{:S(2)}) copy-start(bf16[2,768,512]{2,1,0:T(8,128)(2,1)} %param.3) | copy-start | bytes 4718596

commit v2 on v1

v2 whole, which is shorter than its diff:
```python
import math

import jax
import jax.numpy as jnp
from jax import lax
from jax.experimental import pallas as pl
from jax.experimental.pallas import tpu as pltpu
from jax.sharding import Mesh, PartitionSpec as P

D = 8192
KV = 1024
MICRO = 2
ROWS = 768
USERS_MB = 8
NZ, NX, NY, NC = 8, 4, 8, 2
NU, NT = NZ * NX, NY * NC
WIDTH = D // NT
OUT = KV // NU
TILE = 256
BOUND = 0.3 * math.sqrt(D * KV * ROWS / USERS_MB)
NT_DIMS = (((1,), (1,)), ((), ()))
VMEM_BYTES = 40 * 1024 * 1024


def norms_kernel(x_ref, g_ref, u_ref, out_ref):
    micro = pl.program_id(0)
    users = u_ref[pl.ds(micro, 1), :]
    columns = jnp.transpose(jnp.broadcast_to(users, (8, ROWS)))
    tiles = ROWS // TILE
    sums = [jnp.zeros((1, TILE), jnp.float32) for _ in range(tiles)]
    for i in range(tiles):
        left = pl.ds(i * TILE, TILE)
        for j in range(i, tiles):
            right = pl.ds(j * TILE, TILE)
            xgram = lax.dot_general(x_ref[0, left, :], x_ref[0, right, :], NT_DIMS, preferred_element_type=jnp.float32)
            ggram = lax.dot_general(g_ref[0, left, :], g_ref[0, right, :], NT_DIMS, preferred_element_type=jnp.float32)
            same = columns[i * TILE:(i + 1) * TILE, :1] == users[:, j * TILE:(j + 1) * TILE]
            part = jnp.sum(jnp.where(same, xgram * ggram, 0.0), axis=0, keepdims=True)
            sums[j] = sums[j] + (part if i == j else 2.0 * part)
    total = jnp.concatenate(sums, axis=1)
    labels = lax.broadcasted_iota(jnp.int32, (USERS_MB, ROWS), 0)
    squares = jnp.sum(jnp.where(users == labels, total, 0.0), axis=1, keepdims=True)
    lanes = lax.broadcasted_iota(jnp.int32, (USERS_MB, 128), 1)
    placed = jnp.where(lanes == micro, squares, 0.0)

    @pl.when(micro == 0)
    def _():
        out_ref[...] = jnp.broadcast_to(placed[None], out_ref.shape)

    @pl.when(micro != 0)
    def _():
        out_ref[...] += jnp.broadcast_to(placed[None], out_ref.shape)


def local_norms(activations, key_grads, row_users):
    return pl.pallas_call(
        norms_kernel,
        grid=(MICRO,),
        in_specs=[
            pl.BlockSpec((1, ROWS, WIDTH), lambda m: (m, 0, 0)),
            pl.BlockSpec((1, ROWS, KV), lambda m: (m, 0, 0)),
            pl.BlockSpec((MICRO, ROWS), lambda m: (0, 0)),
        ],
        out_specs=pl.BlockSpec((NT, USERS_MB, 128), lambda m: (0, 0, 0)),
        out_shape=jax.ShapeDtypeStruct((NT, USERS_MB, 128), jnp.float32),
        compiler_params=pltpu.CompilerParams(vmem_limit_bytes=VMEM_BYTES),
        name="norms",
    )(activations, key_grads, row_users)


def flip_kernel(g_ref, out_ref):
    flipped = jnp.transpose(g_ref[0])
    for x in range(NX):
        out_ref[x, 0] = flipped[x * OUT:(x + 1) * OUT, :]


def flip(key_grads):
    return pl.pallas_call(
        flip_kernel,
        grid=(MICRO, NZ),
        in_specs=[pl.BlockSpec((1, ROWS, NX * OUT), lambda m, z: (m, 0, z))],
        out_specs=pl.BlockSpec((NX, 1, OUT, ROWS), lambda m, z: (0, z, 0, m)),
        out_shape=jax.ShapeDtypeStruct((NX, NZ, OUT, MICRO * ROWS), jnp.bfloat16),
        compiler_params=pltpu.CompilerParams(vmem_limit_bytes=VMEM_BYTES),
        name="flip",
    )(key_grads)


def grad_kernel(gt_ref, x_ref, u_ref, sq_ref, out_ref, factor_ref):
    @pl.when(pl.program_id(0) == 0)
    def _():
        squares = jnp.sum(sq_ref[...], axis=0)
        factor = BOUND / jnp.maximum(jnp.sqrt(squares), BOUND)
        labels = lax.broadcasted_iota(jnp.int32, (USERS_MB, ROWS), 0)
        for m in range(MICRO):
            mine = u_ref[m:m + 1, :] == labels
            rows = jnp.sum(jnp.where(mine, factor[:, m:m + 1], 0.0), axis=0, keepdims=True)
            factor_ref[:, m * ROWS:(m + 1) * ROWS] = rows

    gt = gt_ref[0].reshape(NZ * OUT, MICRO * ROWS)
    weighted = (gt.astype(jnp.float32) * factor_ref[...]).astype(jnp.bfloat16)
    total = jnp.dot(weighted, x_ref[...], preferred_element_type=jnp.float32)
    out_ref[0] = total * (1.0 / (MICRO * NU * USERS_MB))


def clipped_grad(flipped, activations, row_users, squares):
    return pl.pallas_call(
        grad_kernel,
        grid=(NX,),
        in_specs=[
            pl.BlockSpec((1, NZ, OUT, MICRO * ROWS), lambda x: (x, 0, 0, 0)),
            pl.BlockSpec((MICRO * ROWS, WIDTH), lambda x: (0, 0)),
            pl.BlockSpec((MICRO, ROWS), lambda x: (0, 0)),
            pl.BlockSpec((NT, USERS_MB, 128), lambda x: (0, 0, 0)),
        ],
        out_specs=pl.BlockSpec((1, NZ * OUT, WIDTH), lambda x: (x, 0, 0)),
        out_shape=jax.ShapeDtypeStruct((NX, NZ * OUT, WIDTH), jnp.float32),
        scratch_shapes=[pltpu.VMEM((1, MICRO * ROWS), jnp.float32)],
        compiler_params=pltpu.CompilerParams(vmem_limit_bytes=VMEM_BYTES),
        name="grad",
    )(flipped, activations.reshape(MICRO * ROWS, WIDTH), row_users, squares)


def body(activations, key_grads, row_users):
    partial = local_norms(activations, key_grads, row_users)
    squares = lax.all_to_all(partial, ("y", "core"), 0, 0)
    flipped = flip(key_grads)
    total = clipped_grad(flipped, activations, row_users, squares)
    total = jnp.sum(lax.all_to_all(total, "x", 0, 0), axis=0)
    total = total.reshape(NZ, OUT, WIDTH)
    return jnp.sum(lax.all_to_all(total, "z", 0, 0), axis=0)


def solution(mesh):
    split = Mesh(mesh.devices.reshape(NZ, NX, NY, NC), ("z", "x", "y", "core"))
    user, tensor = ("z", "x"), ("y", "core")
    return jax.shard_map(
        body,
        mesh=split,
        in_specs=(P(None, user, tensor), P(None, user, None), P(None, user)),
        out_specs=P(user, tensor),
        check_vma=False,
    )
```

time: 85.6 us -> 87 us (1.016)
  matrix products: 10.4 us -> 0 us
  Pallas kernels: 0 us -> 9.24 us
  waiting for transfers between devices: 1.86 us -> 3.24 us
  local copies, waits for them, and re-layouts: 7.78 us -> 8.93 us
    dot_general x7 -> x0, matrix products: 10.4 us -> none  [the longest x2 4.87 us: local_norms(): ggram = jnp.dot(gradient, gradient.T, preferred_element_type=jnp.float32)]
    pallas_call x0 -> x3, Pallas kernels: none -> 9.24 us  [the longest x1 3.8 us: local_norms(): pl.pallas_call(norms_kernel, grid=(MICRO,), in_specs=[pl.BlockSpec((1, RO...]
    unnamed x10 -> x16, local copies, waits for them, and re-layouts: 3.53 us -> 8.93 us
    slice x2 -> x0, local copies, waits for them, and re-layouts: 3.36 us -> none  [the longest x1 3.34 us: body(): key_grads[m]]
    all_to_all x1, waiting for transfers between devices: 1.86 us -> 3.24 us  [body(): squares = lax.all_to_all(partial, ('y', 'core'), 0, 0)]
  transfers between devices with their start and end apart: 1 -> 1, of which waited for: 1 -> 1; matrix products, arithmetic and copies ran while one was open for 7% -> 0% of each run, Pallas kernels for 0% -> 3%
where the time goes in v2:
time: 87 us; the launch traced here: 85.9 us
  blocking collectives  56.4 us (65%)
  Pallas kernels  9.24 us (11%)
  local copies, waits for them, and re-layouts  8.93 us (10%)
  starting transfers between devices  7.2 us (8%)
  waiting for transfers between devices  3.24 us (4%)
  other arithmetic  0.91 us (1%)
    all_to_all x1, blocking collectives, body(): total = jnp.sum(lax.all_to_all(total, 'x', 0, 0), axis=0)  29.6 us
    all_to_all x1, blocking collectives, body(): return jnp.sum(lax.all_to_all(total, 'z', 0, 0), axis=0)  26.7 us
    unnamed x16, local copies, waits for them, and re-layouts  8.93 us
    all_to_all x1, starting transfers between devices, body(): squares = lax.all_to_all(partial, ('y', 'core'), 0, 0)  7.2 us
    pallas_call x1, Pallas kernels, local_norms(): pl.pallas_call(norms_kernel, grid=(MICRO,), in_specs=[pl.BlockSpec((1, RO...  3.8 us
    all_to_all x1, waiting for transfers between devices, body(): squares = lax.all_to_all(partial, ('y', 'core'), 0, 0)  3.24 us
    pallas_call x1, Pallas kernels, flip(): pl.pallas_call(flip_kernel, grid=(MICRO, NZ), in_specs=[pl.BlockSpec((1,...  2.96 us
    pallas_call x1, Pallas kernels, clipped_grad(): pl.pallas_call(grad_kernel, grid=(NX,), in_specs=[pl.BlockSpec((1, NZ, OU...  2.48 us
  transfers between devices with their start and end apart: 1, of which 1 were waited for; matrix products, arithmetic and copies ran while one was open for 0% of the time, Pallas kernels for 3%

profile of v2, /device:TPU:6, one launch (start us, length us, event | category | flops | bytes accessed | tf_op | source)
XLA Modules:
  0.0 85.9 jit_solution(16619250220390553156)
XLA Ops:
  0.0 0.0 copy-start
  0.0 1.9 %copy-done = bf16[2,768,1024]{2,1,0:T(8,128)(2,1)S(1)} copy-done((bf16[2,768,1024]{2,1,0:T(8,128)(2,1)S(1)}, bf16[2,768,1024]{2,1,0:T(8,128)(2,1)}, u32[]{:S(2)}) %copy-start) | copy-done | bytes 3145752
  1.9 0.0 copy-start.4
  1.9 1.4 %copy-done.4 = bf16[2,768,512]{2,1,0:T(8,128)(2,1)S(1)} copy-done((bf16[2,768,512]{2,1,0:T(8,128)(2,1)S(1)}, bf16[2,768,512]{2,1,0:T(8,128)(2,1)}, u32[]{:S(2)}) %copy-start.4) | copy-done | bytes 1572888
  3.3 0.0 copy-start.6
  3.3 0.7 copy-done.6
  4.0 0.0 copy-start.1
  4.0 3.8 %norms.1 = f32[16,8,128]{2,1,0:T(8,128)} custom-call(bf16[2,768,512]{2,1,0:T(8,128)(2,1)S(1)} %copy-done.4, bf16[2,768,1024]{2,1,0:T(8,128)(2,1)S(1)} %copy-done, s32[2,768]{1,0:T(2,128)S(1)} %copy-done.6), custom_call_target="tpu_custom_call" | custom-call | tf_op jit(solution)/shard_map/norms/pallas_call | solution.py:56
  7.8 7.2 %all-to-all-start = ((f32[16,8,128]{2,1,0:T(8,128)}), f32[16,8,128]{2,1,0:T(8,128)S(1)}, u32[]{:S(2)}, u32[]{:S(2)}) async-start(f32[16,8,128]{2,1,0:T(8,128)} %norms.1), calls=%async_computation | async-start | bytes 131072 | tf_op jit(solution)/shard_map/all_to_all | solution.py:126
  15.0 0.0 copy-done.1
  15.0 0.0 copy-start.7
  15.0 3.0 %flip.1.gt_ref = bf16[4,8,32,1536]{3,2,1,0:T(8,128)(2,1)S(1)} custom-call(bf16[2,768,1024]{2,1,0:T(8,128)(2,1)S(1)} %copy-done.1), custom_call_target="tpu_custom_call" | custom-call | tf_op jit(solution)/shard_map/flip/pallas_call | solution.py:78
  18.0 0.0 copy-start.2
  18.0 1.6 %copy-done.2 = bf16[4,8,32,1536]{3,2,1,0:T(8,128)(2,1)} copy-done((bf16[4,8,32,1536]{3,2,1,0:T(8,128)(2,1)}, bf16[4,8,32,1536]{3,2,1,0:T(8,128)(2,1)S(1)}, u32[]{:S(2)}) %copy-start.2) | copy-done | bytes 3145752
  19.6 3.2 %all-to-all-done.sq_ref = f32[16,8,128]{2,1,0:T(8,128)S(1)} async-done(((f32[16,8,128]{2,1,0:T(8,128)}), f32[16,8,128]{2,1,0:T(8,128)S(1)}, u32[]{:S(2)}, u32[]{:S(2)}) %all-to-all-start) | async-done | bytes 65568 | tf_op jit(solution)/shard_map/all_to_all | solution.py:126
  22.9 0.0 copy-done.7
  22.9 0.0 copy-start.3
  22.9 1.9 %copy-done.3 = bf16[4,8,32,1536]{3,2,1,0:T(8,128)(2,1)S(1)} copy-done((bf16[4,8,32,1536]{3,2,1,0:T(8,128)(2,1)S(1)}, bf16[4,8,32,1536]{3,2,1,0:T(8,128)(2,1)}, u32[]{:S(2)}) %copy-start.3) | copy-done | bytes 3145752
  24.8 0.0 copy-start.5
  24.8 1.4 %copy-done.5 = bf16[2,768,512]{2,1,0:T(8,128)(2,1)S(1)} copy-done((bf16[2,768,512]{2,1,0:T(8,128)(2,1)S(1)}, bf16[2,768,512]{2,1,0:T(8,128)(2,1)}, u32[]{:S(2)}) %copy-start.5) | copy-done | bytes 1572888
  26.2 2.5 %grad.1 = f32[4,256,512]{2,1,0:T(8,128)S(1)} custom-call(bf16[4,8,32,1536]{3,2,1,0:T(8,128)(2,1)S(1)} %copy-done.3, bf16[1536,512]{1,0:T(8,128)(2,1)S(1)} %bitcast.2, s32[2,768]{1,0:T(2,128)S(1)} %copy-done.7, f32[16,8,128]{2,1,0:T(8,128)S(1)} %all-to-all-done.sq_ref), custom_call_target="tpu_custom_call" | custom-call | tf_op jit(solution)/shard_map/grad/pallas_call | solution.py:107
  28.7 29.6 %all_to_all.15 = f32[4,256,512]{2,1,0:T(8,128)S(1)} all-to-all(f32[4,256,512]{2,1,0:T(8,128)S(1)} %grad.1), channel_id=1, replica_groups=mesh['z'=8,'x'=4,'y'=8,'core'=2] {'x'}, dimensions={0} | all-to-all | bytes 4194304 | tf_op jit(solution)/shard_map/all_to_all | solution.py:129
  58.3 0.2 reduce_sum.18
  58.5 26.7 %all_to_all.16 = f32[8,32,512]{2,1,0:T(8,128)S(1)} all-to-all(f32[8,32,512]{2,1,0:T(8,128)S(1)} %bitcast.3), channel_id=1, replica_groups=mesh['z'=8,'x'=4,'y'=8,'core'=2] {'z'}, dimensions={0} | all-to-all | bytes 1048576 | tf_op jit(solution)/shard_map/all_to_all | solution.py:131
  85.3 0.7 reduce_sum.19
Async XLA Ops:
  0.0 1.9 %copy-start = (bf16[2,768,1024]{2,1,0:T(8,128)(2,1)S(1)}, bf16[2,768,1024]{2,1,0:T(8,128)(2,1)}, u32[]{:S(2)}) copy-start(bf16[2,768,1024]{2,1,0:T(8,128)(2,1)} %g_ref.3) | copy-start | bytes 9437188
  1.9 1.4 %copy-start.4 = (bf16[2,768,512]{2,1,0:T(8,128)(2,1)S(1)}, bf16[2,768,512]{2,1,0:T(8,128)(2,1)}, u32[]{:S(2)}) copy-start(bf16[2,768,512]{2,1,0:T(8,128)(2,1)} %x_ref.1) | copy-start | bytes 4718596
  3.3 0.7 copy-start.6
  4.0 11.0 %copy-start.1 = (bf16[2,768,1024]{2,1,0:T(8,128)(2,1)S(1)}, bf16[2,768,1024]{2,1,0:T(8,128)(2,1)}, u32[]{:S(2)}) copy-start(bf16[2,768,1024]{2,1,0:T(8,128)(2,1)} %g_ref.3) | copy-start | bytes 9437188
  7.8 15.1 %all-to-all-start = ((f32[16,8,128]{2,1,0:T(8,128)}), f32[16,8,128]{2,1,0:T(8,128)S(1)}, u32[]{:S(2)}, u32[]{:S(2)}) async-start(f32[16,8,128]{2,1,0:T(8,128)} %norms.1), calls=%async_computation | async-start | bytes 131072 | tf_op jit(solution)/shard_map/all_to_all | solution.py:126
  15.0 7.9 %copy-start.7 = (s32[2,768]{1,0:T(2,128)S(1)}, s32[2,768]{1,0:T(2,128)}, u32[]{:S(2)}) copy-start(s32[2,768]{1,0:T(2,128)} %u_ref.3) | copy-start | bytes 18436
  18.0 1.6 %copy-start.2 = (bf16[4,8,32,1536]{3,2,1,0:T(8,128)(2,1)}, bf16[4,8,32,1536]{3,2,1,0:T(8,128)(2,1)S(1)}, u32[]{:S(2)}) copy-start(bf16[4,8,32,1536]{3,2,1,0:T(8,128)(2,1)S(1)} %flip.1.gt_ref) | copy-start | bytes 9437188
  22.9 1.9 %copy-start.3 = (bf16[4,8,32,1536]{3,2,1,0:T(8,128)(2,1)S(1)}, bf16[4,8,32,1536]{3,2,1,0:T(8,128)(2,1)}, u32[]{:S(2)}) copy-start(bf16[4,8,32,1536]{3,2,1,0:T(8,128)(2,1)} %copy-done.2) | copy-start | bytes 9437188
  24.8 1.4 %copy-start.5 = (bf16[2,768,512]{2,1,0:T(8,128)(2,1)S(1)}, bf16[2,768,512]{2,1,0:T(8,128)(2,1)}, u32[]{:S(2)}) copy-start(bf16[2,768,512]{2,1,0:T(8,128)(2,1)} %x_ref.1) | copy-start | bytes 4718596

commit v3 on v2

v3 whole, which is shorter than its diff:
```python
import math

import jax
import jax.numpy as jnp
from jax import lax
from jax.experimental import pallas as pl
from jax.experimental.pallas import tpu as pltpu
from jax.sharding import Mesh, PartitionSpec as P

D = 8192
KV = 1024
MICRO = 2
ROWS = 768
USERS_MB = 8
NZ, NX, NY, NC = 8, 4, 8, 2
NU, NT = NZ * NX, NY * NC
PAIRS = ((0, 1), (3, 2))
CLASSES = ((0, 3), (1, 2))
MEMBERS, DESTS = 4, 8
WIDTH = D // NT
OUT = KV // NU
TILE = 256
BOUND = 0.3 * math.sqrt(D * KV * ROWS / USERS_MB)
NT_DIMS = (((1,), (1,)), ((), ()))
VMEM_BYTES = 60 * 1024 * 1024


def norms_kernel(x_hbm, g_hbm, u_ref, out_ref, x_ref, g_ref, gram_ref, sems):
    tiles = ROWS // TILE
    copies = []
    for m in range(MICRO):
        copies.append((
            pltpu.make_async_copy(g_hbm.at[m], g_ref.at[m], sems.at[0, m]),
            pltpu.make_async_copy(x_hbm.at[m], x_ref.at[m], sems.at[1, m]),
        ))
        for copy in copies[m]:
            copy.start()
    pairs = [(i, j) for j in range(tiles) for i in range(j + 1)]
    placed = jnp.zeros((USERS_MB, 128), jnp.float32)
    for m in range(MICRO):
        users = u_ref[m:m + 1, :]
        columns = jnp.transpose(jnp.broadcast_to(users, (8, ROWS)))
        copies[m][0].wait()
        for at, (i, j) in enumerate(pairs):
            left, right = pl.ds(i * TILE, TILE), pl.ds(j * TILE, TILE)
            ggram = lax.dot_general(g_ref[m, left, :], g_ref[m, right, :], NT_DIMS, preferred_element_type=jnp.float32)
            same = columns[i * TILE:(i + 1) * TILE, :1] == users[:, j * TILE:(j + 1) * TILE]
            gram_ref[at] = jnp.where(same, ggram if i == j else 2.0 * ggram, 0.0)
        copies[m][1].wait()
        sums = [jnp.zeros((1, TILE), jnp.float32) for _ in range(tiles)]
        for at, (i, j) in enumerate(pairs):
            left, right = pl.ds(i * TILE, TILE), pl.ds(j * TILE, TILE)
            xgram = lax.dot_general(x_ref[m, left, :], x_ref[m, right, :], NT_DIMS, preferred_element_type=jnp.float32)
            sums[j] = sums[j] + jnp.sum(xgram * gram_ref[at], axis=0, keepdims=True)
        total = jnp.concatenate(sums, axis=1)
        labels = lax.broadcasted_iota(jnp.int32, (USERS_MB, ROWS), 0)
        squares = jnp.sum(jnp.where(users == labels, total, 0.0), axis=1, keepdims=True)
        lanes = lax.broadcasted_iota(jnp.int32, (USERS_MB, 128), 1)
        placed = placed + jnp.where(lanes == m, squares, 0.0)
    out_ref[...] = jnp.broadcast_to(placed[None], out_ref.shape)


def local_norms(activations, key_grads, row_users):
    return pl.pallas_call(
        norms_kernel,
        in_specs=[
            pl.BlockSpec(memory_space=pltpu.HBM),
            pl.BlockSpec(memory_space=pltpu.HBM),
            pl.BlockSpec(memory_space=pltpu.VMEM),
        ],
        out_specs=pl.BlockSpec(memory_space=pltpu.VMEM),
        out_shape=jax.ShapeDtypeStruct((NT, USERS_MB, 128), jnp.float32),
        scratch_shapes=[
            pltpu.VMEM((MICRO, ROWS, WIDTH), jnp.bfloat16),
            pltpu.VMEM((MICRO, ROWS, KV), jnp.bfloat16),
            pltpu.VMEM((6, TILE, TILE), jnp.float32),
            pltpu.SemaphoreType.DMA((2, MICRO)),
        ],
        compiler_params=pltpu.CompilerParams(vmem_limit_bytes=VMEM_BYTES),
        name="norms",
    )(activations, key_grads, row_users)


def flip_kernel(core_ref, g_hbm, out_hbm, g_ref, out_ref, sems):
    core = core_ref[0]
    reads = [pltpu.make_async_copy(g_hbm.at[m], g_ref.at[m], sems.at[0, m]) for m in range(MICRO)]
    writes = [pltpu.make_async_copy(out_ref.at[k], out_hbm.at[k], sems.at[1, k]) for k in range(MEMBERS)]
    for copy in reads:
        copy.start()
    for m in range(MICRO):
        reads[m].wait()
        for z in range(NZ):
            flipped = jnp.transpose(g_ref[m, :, z * NX * OUT:(z + 1) * NX * OUT])
            zc = lax.rem(z + NZ - core, NZ)
            for x in range(NX):
                xc = lax.rem(x + NX - core, NX)
                inner = jnp.where((xc == 0) | (xc == 3), 0, 1)
                member = 2 * lax.rem(zc, 2) + inner
                dest = 2 * (zc // 2) + xc // 2
                out_ref[member, dest, :, m * ROWS:(m + 1) * ROWS] = flipped[x * OUT:(x + 1) * OUT, :]
    for copy in writes:
        copy.start()
    for copy in writes:
        copy.wait()


def flip(core, key_grads):
    shape = (MEMBERS, DESTS, OUT, MICRO * ROWS)
    return pl.pallas_call(
        flip_kernel,
        in_specs=[pl.BlockSpec(memory_space=pltpu.SMEM), pl.BlockSpec(memory_space=pltpu.HBM)],
        out_specs=pl.BlockSpec(memory_space=pltpu.HBM),
        out_shape=jax.ShapeDtypeStruct(shape, jnp.bfloat16),
        scratch_shapes=[
            pltpu.VMEM((MICRO, ROWS, KV), jnp.bfloat16),
            pltpu.VMEM(shape, jnp.bfloat16),
            pltpu.SemaphoreType.DMA((2, MEMBERS)),
        ],
        compiler_params=pltpu.CompilerParams(vmem_limit_bytes=VMEM_BYTES),
        name="flip",
    )(core, key_grads)


def grad_kernel(gt_hbm, x_hbm, u_ref, sq_ref, out_hbm, gt_ref, x_ref, factor_ref, out_ref, sems):
    inputs = pltpu.make_async_copy(x_hbm, x_ref, sems.at[0, MEMBERS])
    parts = [pltpu.make_async_copy(gt_hbm.at[k], gt_ref.at[k], sems.at[0, k]) for k in range(MEMBERS)]
    writes = [pltpu.make_async_copy(out_ref.at[k], out_hbm.at[k], sems.at[1, k]) for k in range(MEMBERS)]
    inputs.start()
    for copy in parts:
        copy.start()
    squares = jnp.sum(sq_ref[...], axis=0)
    factor = BOUND / jnp.maximum(jnp.sqrt(squares), BOUND)
    labels = lax.broadcasted_iota(jnp.int32, (USERS_MB, ROWS), 0)
    for m in range(MICRO):
        mine = u_ref[m:m + 1, :] == labels
        rows = jnp.sum(jnp.where(mine, factor[:, m:m + 1], 0.0), axis=0, keepdims=True)
        factor_ref[:, m * ROWS:(m + 1) * ROWS] = rows
    for k in range(MEMBERS):
        parts[k].wait()
        gt = gt_ref[k].reshape(DESTS * OUT, MICRO * ROWS)
        weighted = (gt.astype(jnp.float32) * factor_ref[...]).astype(jnp.bfloat16)
        if k == 0:
            inputs.wait()
        inner = x_ref[...].reshape(MICRO * ROWS, WIDTH)
        total = jnp.dot(weighted, inner, preferred_element_type=jnp.float32)
        out_ref[k] = total * (1.0 / (MICRO * NU * USERS_MB))
        writes[k].start()
    for copy in writes:
        copy.wait()


def clipped_grad(flipped, activations, row_users, squares):
    shape = (MEMBERS, DESTS * OUT, WIDTH)
    return pl.pallas_call(
        grad_kernel,
        in_specs=[
            pl.BlockSpec(memory_space=pltpu.HBM),
            pl.BlockSpec(memory_space=pltpu.HBM),
            pl.BlockSpec(memory_space=pltpu.VMEM),
            pl.BlockSpec(memory_space=pltpu.VMEM),
        ],
        out_specs=pl.BlockSpec(memory_space=pltpu.HBM),
        out_shape=jax.ShapeDtypeStruct(shape, jnp.float32),
        scratch_shapes=[
            pltpu.VMEM((MEMBERS, DESTS, OUT, MICRO * ROWS), jnp.bfloat16),
            pltpu.VMEM((MICRO, ROWS, WIDTH), jnp.bfloat16),
            pltpu.VMEM((1, MICRO * ROWS), jnp.float32),
            pltpu.VMEM(shape, jnp.float32),
            pltpu.SemaphoreType.DMA((2, MEMBERS + 1)),
        ],
        compiler_params=pltpu.CompilerParams(vmem_limit_bytes=VMEM_BYTES),
        name="grad",
    )(flipped, activations, row_users, squares)


def place(zc, xc, core):
    return ((zc + core) % NZ * NX + (xc + core) % NX) * NC + core


def stage_groups():
    first = [
        [place(2 * k + b, x, core) for b in range(2) for x in pair]
        for core in range(NC) for k in range(NZ // 2) for pair in PAIRS
    ]
    second = [
        [place(2 * k + b, x, core) for k in range(NZ // 2) for x in group]
        for core in range(NC) for b in range(2) for group in CLASSES
    ]
    return first, second


def body(activations, key_grads, row_users):
    partial = local_norms(activations, key_grads, row_users)
    squares = lax.all_to_all(partial, ("y", "core"), 0, 0)
    core = jnp.full((1,), lax.axis_index("core"), jnp.int32)
    total = clipped_grad(flip(core, key_grads), activations, row_users, squares)
    first, second = stage_groups()
    axes = ("z", "x", "core")
    total = jnp.sum(lax.all_to_all(total, axes, 0, 0, axis_index_groups=first), axis=0)
    total = total.reshape(DESTS, OUT, WIDTH)
    return jnp.sum(lax.all_to_all(total, axes, 0, 0, axis_index_groups=second), axis=0)


def solution(mesh):
    split = Mesh(mesh.devices.reshape(NZ, NX, NY, NC), ("z", "x", "y", "core"))
    user, tensor = ("z", "x"), ("y", "core")
    return jax.shard_map(
        body,
        mesh=split,
        in_specs=(P(None, user, tensor), P(None, user, None), P(None, user)),
        out_specs=P(user, tensor),
        check_vma=False,
    )
```

time: 87 us -> 77.3 us (0.89)
  the two profiles are of different devices: /device:TPU:6 before, /device:TPU:3 now
where the time goes in v3:
time: 77.3 us; the launch traced here: 76.9 us
  blocking collectives  47.5 us (61%)
  Pallas kernels  16.3 us (21%)
  starting transfers between devices  7.8 us (10%)
  waiting for transfers between devices  3.72 us (5%)
  other arithmetic  0.91 us (1%)
    all_to_all x1, blocking collectives, body(): lax.all_to_all(total, axes, 0, 0, axis_index_groups=first)  25.9 us
    all_to_all x1, blocking collectives, body(): lax.all_to_all(total, axes, 0, 0, axis_index_groups=second)  21.6 us
    all_to_all x1, starting transfers between devices, body(): squares = lax.all_to_all(partial, ('y', 'core'), 0, 0)  7.8 us
    pallas_call x1, Pallas kernels, local_norms(): pl.pallas_call(norms_kernel, in_specs=[pl.BlockSpec(memory_space=pltpu.HB...  6.24 us
    pallas_call x1, Pallas kernels, clipped_grad(): pl.pallas_call(grad_kernel, in_specs=[pl.BlockSpec(memory_space=pltpu.HBM...  6 us
    pallas_call x1, Pallas kernels, flip(): pl.pallas_call(flip_kernel, in_specs=[pl.BlockSpec(memory_space=pltpu.SME...  4.08 us
    all_to_all x1, waiting for transfers between devices, body(): squares = lax.all_to_all(partial, ('y', 'core'), 0, 0)  3.72 us
  transfers between devices with their start and end apart: 1, of which 1 were waited for; matrix products, arithmetic and copies ran while one was open for 0% of the time, Pallas kernels for 5%

profile of v3, /device:TPU:3, one launch (start us, length us, event | category | flops | bytes accessed | tf_op | source)
XLA Modules:
  0.0 76.9 jit_solution(1958751792910886512)
XLA Ops:
  0.0 6.2 %norms.1 = f32[16,8,128]{2,1,0:T(8,128)} custom-call(bf16[2,768,512]{2,1,0:T(8,128)(2,1)} %x_hbm.3, bf16[2,768,1024]{2,1,0:T(8,128)(2,1)} %g_hbm.3, s32[2,768]{1,0:T(2,128)} %u_ref.3), custom_call_target="tpu_custom_call" | custom-call | tf_op jit(solution)/shard_map/norms/pallas_call | solution.py:64
  6.3 7.8 %all-to-all-start = ((f32[16,8,128]{2,1,0:T(8,128)}), f32[16,8,128]{2,1,0:T(8,128)S(1)}, u32[]{:S(2)}, u32[]{:S(2)}) async-start(f32[16,8,128]{2,1,0:T(8,128)} %norms.1), calls=%async_computation | async-start | bytes 131072 | tf_op jit(solution)/shard_map/all_to_all | solution.py:194
  14.1 4.1 %flip.1.gt_hbm = bf16[4,8,32,1536]{3,2,1,0:T(8,128)(2,1)} custom-call(s32[1]{0:T(128)} %bitcast.core_ref, bf16[2,768,1024]{2,1,0:T(8,128)(2,1)} %g_hbm.3), custom_call_target="tpu_custom_call" | custom-call | tf_op jit(solution)/shard_map/flip/pallas_call | solution.py:109
  18.1 3.7 %all-to-all-done.sq_ref = f32[16,8,128]{2,1,0:T(8,128)S(1)} async-done(((f32[16,8,128]{2,1,0:T(8,128)}), f32[16,8,128]{2,1,0:T(8,128)S(1)}, u32[]{:S(2)}, u32[]{:S(2)}) %all-to-all-start) | async-done | bytes 65568 | tf_op jit(solution)/shard_map/all_to_all | solution.py:194
  21.9 0.0 copy-start
  21.9 0.6 copy-done
  22.5 6.0 %grad.1 = f32[4,256,512]{2,1,0:T(8,128)} custom-call(bf16[4,8,32,1536]{3,2,1,0:T(8,128)(2,1)} %flip.1.gt_hbm, bf16[2,768,512]{2,1,0:T(8,128)(2,1)} %x_hbm.3, s32[2,768]{1,0:T(2,128)} %u_ref.3, f32[16,8,128]{2,1,0:T(8,128)} %copy-done), custom_call_target="tpu_custom_call" | custom-call | tf_op jit(solution)/shard_map/grad/pallas_call | solution.py:154
  28.5 25.9 %all_to_all.15 = f32[4,256,512]{2,1,0:T(8,128)S(1)} all-to-all(f32[4,256,512]{2,1,0:T(8,128)} %grad.1), channel_id=1, replica_groups={{0,16,64,80},{48,32,112,96},{128,144,192,208},{176,160,240,224},{256,27..., dimensions={0} | all-to-all | bytes 4194304 | tf_op jit(solution)/shard_map/all_to_all | solution.py:199
  54.4 0.2 reduce_sum.18
  54.7 21.6 %all_to_all.16 = f32[8,32,512]{2,1,0:T(8,128)S(1)} all-to-all(f32[8,32,512]{2,1,0:T(8,128)S(1)} %bitcast.2), channel_id=1, replica_groups={{0,48,128,176,256,304,384,432},{16,32,144,160,272,288,400,416},{64,112,..., dimensions={0} | all-to-all | bytes 1048576 | tf_op jit(solution)/shard_map/all_to_all | solution.py:201
  76.3 0.7 reduce_sum.19
Async XLA Ops:
  6.3 15.6 %all-to-all-start = ((f32[16,8,128]{2,1,0:T(8,128)}), f32[16,8,128]{2,1,0:T(8,128)S(1)}, u32[]{:S(2)}, u32[]{:S(2)}) async-start(f32[16,8,128]{2,1,0:T(8,128)} %norms.1), calls=%async_computation | async-start | bytes 131072 | tf_op jit(solution)/shard_map/all_to_all | solution.py:194
  21.9 0.6 copy-start

commit v4 on v3

v4 whole, which is shorter than its diff:
```python
import functools
import math

import jax
import jax.numpy as jnp
from jax import lax
from jax.experimental import pallas as pl
from jax.experimental.pallas import tpu as pltpu
from jax.sharding import Mesh, PartitionSpec as P

D = 8192
KV = 1024
MICRO = 2
ROWS = 768
USERS_MB = 8
NZ, NX, NY, NC = 8, 4, 8, 2
NU, NT = NZ * NX, NY * NC
SENT = (3, 1, 2)
CLASSES = ((0, 3), (1, 2))
MEMBERS, DESTS = 4, 8
WIDTH = D // NT
OUT = KV // NU
TILE = 256
LANES = 128
BOUND = 0.3 * math.sqrt(D * KV * ROWS / USERS_MB)
NT_DIMS = (((1,), (1,)), ((), ()))
VMEM_BYTES = 60 * 1024 * 1024


def norms_kernel(x_ref, g_ref, u_ref, out_ref):
    micro = pl.program_id(0)
    x, g = x_ref[0], g_ref[0]
    users = u_ref[pl.ds(micro, 1), :]
    columns = jnp.transpose(jnp.broadcast_to(users, (8, ROWS)))[:, :1]
    sums = []
    for first in range(0, ROWS, TILE):
        last = first + TILE
        xgram = lax.dot_general(x[:last], x[first:last], NT_DIMS, preferred_element_type=jnp.float32)
        ggram = lax.dot_general(g[:last], g[first:last], NT_DIMS, preferred_element_type=jnp.float32)
        both = jnp.where(columns[:last] == users[:, first:last], xgram * ggram, 0.0)
        total = jnp.sum(both[first:], axis=0, keepdims=True)
        if first:
            total = total + 2.0 * jnp.sum(both[:first], axis=0, keepdims=True)
        sums.append(total)
    total = jnp.concatenate(sums, axis=1)
    labels = lax.broadcasted_iota(jnp.int32, (USERS_MB, ROWS), 0)
    squares = jnp.sum(jnp.where(users == labels, total, 0.0), axis=1, keepdims=True)
    lanes = lax.broadcasted_iota(jnp.int32, (USERS_MB, LANES), 1)
    slots = lax.broadcasted_iota(jnp.int32, (USERS_MB, LANES), 0) + micro * USERS_MB
    placed = jnp.sum(jnp.where(lanes == slots, squares, 0.0), axis=0, keepdims=True)

    @pl.when(micro == 0)
    def _():
        out_ref[...] = jnp.broadcast_to(placed[None], out_ref.shape)

    @pl.when(micro != 0)
    def _():
        out_ref[...] += jnp.broadcast_to(placed[None], out_ref.shape)


def local_norms(activations, key_grads, row_users):
    return pl.pallas_call(
        norms_kernel,
        grid=(MICRO,),
        in_specs=[
            pl.BlockSpec((1, ROWS, WIDTH), lambda m: (m, 0, 0)),
            pl.BlockSpec((1, ROWS, KV), lambda m: (m, 0, 0)),
            pl.BlockSpec((MICRO, ROWS), lambda m: (0, 0)),
        ],
        out_specs=pl.BlockSpec((NT, 1, LANES), lambda m: (0, 0, 0)),
        out_shape=jax.ShapeDtypeStruct((NT, 1, LANES), jnp.float32),
        compiler_params=pltpu.CompilerParams(vmem_limit_bytes=VMEM_BYTES),
        name="norms",
    )(activations, key_grads, row_users)


def my_place():
    core = lax.axis_index("core")
    zc = lax.rem(lax.axis_index("z") + NZ - core, NZ)
    xc = lax.rem(lax.axis_index("x") + NX - core, NX)
    return core, 2 * lax.rem(zc, 2) + inner_class(xc)


def inner_class(xc):
    return jnp.where((xc == 0) | (xc == 3), 0, 1)


def flip_kernel(g_hbm, out_hbm, g_ref, out_ref, sems):
    core, own = my_place()
    reads = [pltpu.make_async_copy(g_hbm.at[m], g_ref.at[m], sems.at[0, m]) for m in range(MICRO)]
    writes = [pltpu.make_async_copy(out_ref.at[k], out_hbm.at[k], sems.at[1, k]) for k in range(MEMBERS)]
    for copy in reads:
        copy.start()
    for m in range(MICRO):
        reads[m].wait()
        for z in range(NZ):
            flipped = jnp.transpose(g_ref[m, :, z * NX * OUT:(z + 1) * NX * OUT])
            zc = lax.rem(z + NZ - core, NZ)
            for x in range(NX):
                xc = lax.rem(x + NX - core, NX)
                member = lax.bitwise_xor(2 * lax.rem(zc, 2) + inner_class(xc), own)
                dest = 2 * (zc // 2) + xc // 2
                out_ref[member, dest, :, m * ROWS:(m + 1) * ROWS] = flipped[x * OUT:(x + 1) * OUT, :]
    for copy in writes:
        copy.start()
    for copy in writes:
        copy.wait()


def flip(key_grads):
    shape = (MEMBERS, DESTS, OUT, MICRO * ROWS)
    return pl.pallas_call(
        flip_kernel,
        in_specs=[pl.BlockSpec(memory_space=pltpu.HBM)],
        out_specs=pl.BlockSpec(memory_space=pltpu.HBM),
        out_shape=jax.ShapeDtypeStruct(shape, jnp.bfloat16),
        scratch_shapes=[
            pltpu.VMEM((MICRO, ROWS, KV), jnp.bfloat16),
            pltpu.VMEM(shape, jnp.bfloat16),
            pltpu.SemaphoreType.DMA((2, MEMBERS)),
        ],
        compiler_params=pltpu.CompilerParams(vmem_limit_bytes=VMEM_BYTES),
        name="flip",
    )(key_grads)


def grad_kernel(members, gt_hbm, x_hbm, u_hbm, sq_ref, *rest):
    count = len(members)
    out_hbm = rest[:count]
    gt_ref, x_ref, u_ref, factor_ref, out_ref, sems = rest[count:]
    small = [pltpu.make_async_copy(u_hbm, u_ref, sems.at[2, 0])]
    inputs = [pltpu.make_async_copy(x_hbm.at[m], x_ref.at[m], sems.at[2, 2 + m]) for m in range(MICRO)]
    parts = [pltpu.make_async_copy(gt_hbm.at[k], gt_ref.at[at], sems.at[0, at]) for at, k in enumerate(members)]
    writes = [pltpu.make_async_copy(out_ref.at[at], out_hbm[at], sems.at[1, at]) for at in range(count)]
    for copy in small + parts[:1] + inputs + parts[1:]:
        copy.start()
    for copy in small:
        copy.wait()
    squares = jnp.sum(sq_ref[...], axis=0)
    factor = BOUND / jnp.maximum(jnp.sqrt(squares), BOUND)
    lanes = lax.broadcasted_iota(jnp.int32, (USERS_MB, LANES), 1)
    slots = lax.broadcasted_iota(jnp.int32, (USERS_MB, LANES), 0)
    labels = lax.broadcasted_iota(jnp.int32, (USERS_MB, ROWS), 0)
    for m in range(MICRO):
        column = jnp.sum(jnp.where(lanes == slots + m * USERS_MB, factor, 0.0), axis=1, keepdims=True)
        rows = jnp.sum(jnp.where(u_ref[m:m + 1, :] == labels, column, 0.0), axis=0, keepdims=True)
        factor_ref[:, m * ROWS:(m + 1) * ROWS] = rows
    for at in range(count):
        parts[at].wait()
        gt = gt_ref[at].reshape(DESTS * OUT, MICRO * ROWS)
        weighted = (gt.astype(jnp.float32) * factor_ref[...]).astype(jnp.bfloat16)
        if at == 0:
            for copy in inputs:
                copy.wait()
        inner = x_ref[...].reshape(MICRO * ROWS, WIDTH)
        total = jnp.dot(weighted, inner, preferred_element_type=jnp.float32)
        out_ref[at] = total * (1.0 / (MICRO * NU * USERS_MB))
        writes[at].start()
    for copy in writes:
        copy.wait()


def clipped_grad(members, flipped, activations, row_users, squares, vmem_bytes=VMEM_BYTES):
    count = len(members)
    shape = (DESTS * OUT, WIDTH)
    return pl.pallas_call(
        functools.partial(grad_kernel, members),
        in_specs=[pl.BlockSpec(memory_space=pltpu.HBM)] * 3 + [pl.BlockSpec(memory_space=pltpu.VMEM)],
        out_specs=[pl.BlockSpec(memory_space=pltpu.HBM)] * count,
        out_shape=[jax.ShapeDtypeStruct(shape, jnp.float32)] * count,
        scratch_shapes=[
            pltpu.VMEM((count, DESTS, OUT, MICRO * ROWS), jnp.bfloat16),
            pltpu.VMEM((MICRO, ROWS, WIDTH), jnp.bfloat16),
            pltpu.VMEM((MICRO, ROWS), jnp.int32),
            pltpu.VMEM((1, MICRO * ROWS), jnp.float32),
            pltpu.VMEM((count,) + shape, jnp.float32),
            pltpu.SemaphoreType.DMA((3, MEMBERS)),
        ],
        compiler_params=pltpu.CompilerParams(vmem_limit_bytes=vmem_bytes),
        name="grad",
    )(flipped, activations, row_users, squares)


def place(zc, xc, core):
    return ((zc + core) % NZ * NX + (xc + core) % NX) * NC + core


def stage_groups():
    first = [
        [(place(z, x, core), place(z ^ (k // 2), x ^ (k % 2), core)) for core in range(NC) for z in range(NZ) for x in range(NX)]
        for k in range(MEMBERS)
    ]
    second = [
        [place(2 * k + b, x, core) for k in range(NZ // 2) for x in group]
        for core in range(NC) for b in range(2) for group in CLASSES
    ]
    return first, second


def body(activations, key_grads, row_users):
    partial = local_norms(activations, key_grads, row_users)
    squares = lax.all_to_all(partial, ("y", "core"), 0, 0)
    flipped = flip(key_grads)
    first, second = stage_groups()
    axes = ("z", "x", "core")
    sent = clipped_grad(SENT, flipped, activations, row_users, squares, 52 * 1024 * 1024)
    kept, = clipped_grad((0,), flipped, activations, row_users, squares, 16 * 1024 * 1024)
    got = [lax.ppermute(part, axes, first[k]) for k, part in zip(SENT, sent)]
    total = kept + got[0] + got[1] + got[2]
    total = total.reshape(DESTS, OUT, WIDTH)
    return jnp.sum(lax.all_to_all(total, axes, 0, 0, axis_index_groups=second), axis=0)


def solution(mesh):
    split = Mesh(mesh.devices.reshape(NZ, NX, NY, NC), ("z", "x", "y", "core"))
    user, tensor = ("z", "x"), ("y", "core")
    return jax.shard_map(
        body,
        mesh=split,
        in_specs=(P(None, user, tensor), P(None, user, None), P(None, user)),
        out_specs=P(user, tensor),
        check_vma=False,
    )
```

time: 77.3 us -> 71.6 us (0.926)
  the two profiles are of different devices: /device:TPU:3 before, /device:TPU:6 now
where the time goes in v4:
time: 71.6 us; the launch traced here: 70.8 us
  blocking collectives  27.4 us (38%)
  starting transfers between devices  16.8 us (23%)
  Pallas kernels  14.4 us (20%)
  waiting for transfers between devices  11.2 us (16%)
  other arithmetic  0.88 us (1%)
    all_to_all x1, blocking collectives, body(): lax.all_to_all(total, axes, 0, 0, axis_index_groups=second)  27.4 us
    ppermute x3, starting transfers between devices, body(): got = [lax.ppermute(part, axes, first[k]) for k, part in zip(SENT, sent)]  9.57 us
    ppermute x3, waiting for transfers between devices, body(): got = [lax.ppermute(part, axes, first[k]) for k, part in zip(SENT, sent)]  7.8 us
    all_to_all x1, starting transfers between devices, body(): squares = lax.all_to_all(partial, ('y', 'core'), 0, 0)  7.21 us
    pallas_call x1, Pallas kernels, local_norms(): pl.pallas_call(norms_kernel, grid=(MICRO,), in_specs=[pl.BlockSpec((1, RO...  5.32 us
    pallas_call x2, Pallas kernels, clipped_grad(): pl.pallas_call(functools.partial(grad_kernel, members), in_specs=[pl.Bloc...  5 us
    pallas_call x1, Pallas kernels, flip(): pl.pallas_call(flip_kernel, in_specs=[pl.BlockSpec(memory_space=pltpu.HBM...  4.07 us
    all_to_all x1, waiting for transfers between devices, body(): squares = lax.all_to_all(partial, ('y', 'core'), 0, 0)  3.4 us
  transfers between devices with their start and end apart: 4, of which 4 were waited for; matrix products, arithmetic and copies ran while one was open for 0% of the time, Pallas kernels for 8%

profile of v4, /device:TPU:6, one launch (start us, length us, event | category | flops | bytes accessed | tf_op | source)
XLA Modules:
  0.0 70.8 jit_solution(16223768777147030720)
XLA Ops:
  0.0 5.3 %norms.1 = f32[16,1,128]{2,1,0:T(1,128)} custom-call(bf16[2,768,512]{2,1,0:T(8,128)(2,1)} %x_hbm.3, bf16[2,768,1024]{2,1,0:T(8,128)(2,1)} %g_ref.1, s32[2,768]{1,0:T(2,128)} %u_hbm.3), custom_call_target="tpu_custom_call" | custom-call | tf_op jit(solution)/shard_map/norms/pallas_call | solution.py:62
  5.3 7.2 %all-to-all-start = ((f32[16,1,128]{2,1,0:T(1,128)}), f32[16,1,128]{2,1,0:T(1,128)S(1)}, u32[]{:S(2)}, u32[]{:S(2)}) async-start(f32[16,1,128]{2,1,0:T(1,128)} %norms.1), calls=%async_computation | async-start | bytes 16384 | tf_op jit(solution)/shard_map/all_to_all | solution.py:202
  12.5 0.0 copy-start.2
  12.5 4.1 %flip.1.gt_hbm = bf16[4,8,32,1536]{3,2,1,0:T(8,128)(2,1)} custom-call(bf16[2,768,1024]{2,1,0:T(8,128)(2,1)} %g_ref.1), custom_call_target="tpu_custom_call" | custom-call | tf_op jit(solution)/shard_map/flip/pallas_call | solution.py:112
  16.6 0.0 copy-start
  16.6 3.4 %all-to-all-done.sq_ref = f32[16,1,128]{2,1,0:T(1,128)S(1)} async-done(((f32[16,1,128]{2,1,0:T(1,128)}), f32[16,1,128]{2,1,0:T(1,128)S(1)}, u32[]{:S(2)}, u32[]{:S(2)}) %all-to-all-start) | async-done | bytes 8224 | tf_op jit(solution)/shard_map/all_to_all | solution.py:202
  20.0 0.0 copy-done.2
  20.0 0.0 copy-start.1
  20.0 3.7 %grad.3 = (f32[256,512]{1,0:T(8,128)S(1)}, f32[256,512]{1,0:T(8,128)S(1)}, f32[256,512]{1,0:T(8,128)S(1)}) custom-call(bf16[4,8,32,1536]{3,2,1,0:T(8,128)(2,1)} %flip.1.gt_hbm, bf16[2,768,512]{2,1,0:T(8,128)(2,1)} %x_hbm.3, s32[2,768]{1,0:T(2,128)S(1)} %copy-done.2, f32[16,1,128]{2,1,0:T(1,128)S(1)} %all-to-all-done.sq_ref), custom_call_target="tpu_custom_call" | custom-call | tf_op jit(solution)/shard_map/grad/pallas_call | solution.py:166
  23.7 4.5 %collective-permute-start = (f32[256,512]{1,0:T(8,128)S(1)}, f32[256,512]{1,0:T(8,128)S(1)}, u32[]{:S(2)}, u32[]{:S(2)}) collective-permute-start(f32[256,512]{1,0:T(8,128)S(1)} %get-tuple-element.8), channel_id=1, source_target_pairs={{0,80},{16,64},{32,112},{48,96},{64,16},{80,0},{96,48},{112,32},{1... | collective-permute-start | bytes 1572872 | tf_op jit(solution)/shard_map/ppermute | solution.py:208
  28.3 3.1 %collective-permute-start.1 = (f32[256,512]{1,0:T(8,128)S(1)}, f32[256,512]{1,0:T(8,128)S(1)}, u32[]{:S(2)}, u32[]{:S(2)}) collective-permute-start(f32[256,512]{1,0:T(8,128)S(1)} %get-tuple-element.9), channel_id=1, source_target_pairs={{0,16},{16,0},{32,48},{48,32},{64,80},{80,64},{96,112},{112,96},{1... | collective-permute-start | bytes 1572872 | tf_op jit(solution)/shard_map/ppermute | solution.py:208
  31.4 1.9 %collective-permute-start.2 = (f32[256,512]{1,0:T(8,128)S(1)}, f32[256,512]{1,0:T(8,128)S(1)}, u32[]{:S(2)}, u32[]{:S(2)}) collective-permute-start(f32[256,512]{1,0:T(8,128)S(1)} %get-tuple-element.10), channel_id=1, source_target_pairs={{0,64},{16,80},{32,96},{48,112},{64,0},{80,16},{96,32},{112,48},{1... | collective-permute-start | bytes 1572872 | tf_op jit(solution)/shard_map/ppermute | solution.py:208
  33.3 0.0 copy-done
  33.3 0.0 copy-done.1
  33.3 1.3 %grad.2 = f32[256,512]{1,0:T(8,128)S(1)} custom-call(bf16[4,8,32,1536]{3,2,1,0:T(8,128)(2,1)S(1)} %copy-done, bf16[2,768,512]{2,1,0:T(8,128)(2,1)S(1)} %copy-done.1, s32[2,768]{1,0:T(2,128)S(1)} %copy-done.2, f32[16,1,128]{2,1,0:T(1,128)S(1)} %all-to-all-done.sq_ref), custom_call_target="tpu_custom_call" | custom-call | tf_op jit(solution)/shard_map/grad/pallas_call | solution.py:166
  34.7 1.1 %collective-permute-done = f32[256,512]{1,0:T(8,128)S(1)} collective-permute-done((f32[256,512]{1,0:T(8,128)S(1)}, f32[256,512]{1,0:T(8,128)S(1)}, u32[]{:S(2)}, u32[]{:S(2)}) %collective-permute-start) | collective-permute-done | bytes 524320 | tf_op jit(solution)/shard_map/ppermute | solution.py:208
  35.8 5.5 %collective-permute-done.1 = f32[256,512]{1,0:T(8,128)S(1)} collective-permute-done((f32[256,512]{1,0:T(8,128)S(1)}, f32[256,512]{1,0:T(8,128)S(1)}, u32[]{:S(2)}, u32[]{:S(2)}) %collective-permute-start.1) | collective-permute-done | bytes 524320 | tf_op jit(solution)/shard_map/ppermute | solution.py:208
  41.3 1.1 %collective-permute-done.2 = f32[256,512]{1,0:T(8,128)S(1)} collective-permute-done((f32[256,512]{1,0:T(8,128)S(1)}, f32[256,512]{1,0:T(8,128)S(1)}, u32[]{:S(2)}, u32[]{:S(2)}) %collective-permute-start.2) | collective-permute-done | bytes 524320 | tf_op jit(solution)/shard_map/ppermute | solution.py:208
  42.5 0.2 add_add_fusion
  42.7 27.4 %all_to_all.10 = f32[8,32,512]{2,1,0:T(8,128)S(1)} all-to-all(f32[8,32,512]{2,1,0:T(8,128)S(1)} %bitcast.1), channel_id=1, replica_groups={{0,48,128,176,256,304,384,432},{16,32,144,160,272,288,400,416},{64,112,..., dimensions={0} | all-to-all | bytes 1048576 | tf_op jit(solution)/shard_map/all_to_all | solution.py:211
  70.1 0.7 reduce_sum.9
Async XLA Ops:
  5.3 14.7 %all-to-all-start = ((f32[16,1,128]{2,1,0:T(1,128)}), f32[16,1,128]{2,1,0:T(1,128)S(1)}, u32[]{:S(2)}, u32[]{:S(2)}) async-start(f32[16,1,128]{2,1,0:T(1,128)} %norms.1), calls=%async_computation | async-start | bytes 16384 | tf_op jit(solution)/shard_map/all_to_all | solution.py:202
  12.5 7.5 %copy-start.2 = (s32[2,768]{1,0:T(2,128)S(1)}, s32[2,768]{1,0:T(2,128)}, u32[]{:S(2)}) copy-start(s32[2,768]{1,0:T(2,128)} %u_hbm.3) | copy-start | bytes 18436
  16.6 16.7 %copy-start = (bf16[4,8,32,1536]{3,2,1,0:T(8,128)(2,1)S(1)}, bf16[4,8,32,1536]{3,2,1,0:T(8,128)(2,1)}, u32[]{:S(2)}) copy-start(bf16[4,8,32,1536]{3,2,1,0:T(8,128)(2,1)} %flip.1.gt_hbm) | copy-start | bytes 9437188
  20.0 13.3 %copy-start.1 = (bf16[2,768,512]{2,1,0:T(8,128)(2,1)S(1)}, bf16[2,768,512]{2,1,0:T(8,128)(2,1)}, u32[]{:S(2)}) copy-start(bf16[2,768,512]{2,1,0:T(8,128)(2,1)} %x_hbm.3) | copy-start | bytes 4718596
  23.7 12.1 %collective-permute-start = (f32[256,512]{1,0:T(8,128)S(1)}, f32[256,512]{1,0:T(8,128)S(1)}, u32[]{:S(2)}, u32[]{:S(2)}) collective-permute-start(f32[256,512]{1,0:T(8,128)S(1)} %get-tuple-element.8), channel_id=1, source_target_pairs={{0,80},{16,64},{32,112},{48,96},{64,16},{80,0},{96,48},{112,32},{1... | collective-permute-start | bytes 1572872 | tf_op jit(solution)/shard_map/ppermute | solution.py:208
  28.3 13.0 %collective-permute-start.1 = (f32[256,512]{1,0:T(8,128)S(1)}, f32[256,512]{1,0:T(8,128)S(1)}, u32[]{:S(2)}, u32[]{:S(2)}) collective-permute-start(f32[256,512]{1,0:T(8,128)S(1)} %get-tuple-element.9), channel_id=1, source_target_pairs={{0,16},{16,0},{32,48},{48,32},{64,80},{80,64},{96,112},{112,96},{1... | collective-permute-start | bytes 1572872 | tf_op jit(solution)/shard_map/ppermute | solution.py:208
  31.4 11.1 %collective-permute-start.2 = (f32[256,512]{1,0:T(8,128)S(1)}, f32[256,512]{1,0:T(8,128)S(1)}, u32[]{:S(2)}, u32[]{:S(2)}) collective-permute-start(f32[256,512]{1,0:T(8,128)S(1)} %get-tuple-element.10), channel_id=1, source_target_pairs={{0,64},{16,80},{32,96},{48,112},{64,0},{80,16},{96,32},{112,48},{1... | collective-permute-start | bytes 1572872 | tf_op jit(solution)/shard_map/ppermute | solution.py:208

commit v5 on v4

--- a/solution.py
+++ b/solution.py
@@ -16,7 +16,8 @@
 NZ, NX, NY, NC = 8, 4, 8, 2
 NU, NT = NZ * NX, NY * NC
 SENT = (3, 1, 2)
-CLASSES = ((0, 3), (1, 2))
+Z_CLASSES = ((0, 2, 5, 7), (1, 3, 4, 6))
+X_CLASSES = ((0, 3), (1, 2))
 MEMBERS, DESTS = 4, 8
 WIDTH = D // NT
 OUT = KV // NU
@@ -78,11 +79,12 @@
     core = lax.axis_index("core")
     zc = lax.rem(lax.axis_index("z") + NZ - core, NZ)
     xc = lax.rem(lax.axis_index("x") + NX - core, NX)
-    return core, 2 * lax.rem(zc, 2) + inner_class(xc)
-
-
-def inner_class(xc):
-    return jnp.where((xc == 0) | (xc == 3), 0, 1)
+    return core, class_of(zc, xc)
+
+
+def class_of(zc, xc):
+    along_z = lax.bitwise_xor(lax.rem(zc, 2), zc // 4)
+    return 2 * along_z + jnp.where((xc == 0) | (xc == 3), 0, 1)
 
 
 def flip_kernel(g_hbm, out_hbm, g_ref, out_ref, sems):
@@ -98,7 +100,7 @@
             zc = lax.rem(z + NZ - core, NZ)
             for x in range(NX):
                 xc = lax.rem(x + NX - core, NX)
-                member = lax.bitwise_xor(2 * lax.rem(zc, 2) + inner_class(xc), own)
+                member = lax.bitwise_xor(class_of(zc, xc), own)
                 dest = 2 * (zc // 2) + xc // 2
                 out_ref[member, dest, :, m * ROWS:(m + 1) * ROWS] = flipped[x * OUT:(x + 1) * OUT, :]
     for copy in writes:
@@ -191,8 +193,8 @@
         for k in range(MEMBERS)
     ]
     second = [
-        [place(2 * k + b, x, core) for k in range(NZ // 2) for x in group]
-        for core in range(NC) for b in range(2) for group in CLASSES
+        [place(z, x, core) for z in along_z for x in along_x]
+        for core in range(NC) for along_z in Z_CLASSES for along_x in X_CLASSES
     ]
     return first, second
 

time: 71.6 us -> 69.5 us (0.971)
  blocking collectives: 27.4 us -> 25.7 us
    all_to_all x1, blocking collectives: 27.4 us -> 25.7 us  [body(): lax.all_to_all(total, axes, 0, 0, axis_index_groups=second)]
where the time goes in v5:
time: 69.5 us; the launch traced here: 69 us
  blocking collectives  25.7 us (37%)
  starting transfers between devices  16.8 us (24%)
  Pallas kernels  14.4 us (21%)
  waiting for transfers between devices  11.2 us (16%)
  other arithmetic  0.88 us (1%)
    all_to_all x1, blocking collectives, body(): lax.all_to_all(total, axes, 0, 0, axis_index_groups=second)  25.7 us
    ppermute x3, starting transfers between devices, body(): got = [lax.ppermute(part, axes, first[k]) for k, part in zip(SENT, sent)]  9.57 us
    ppermute x3, waiting for transfers between devices, body(): got = [lax.ppermute(part, axes, first[k]) for k, part in zip(SENT, sent)]  7.8 us
    all_to_all x1, starting transfers between devices, body(): squares = lax.all_to_all(partial, ('y', 'core'), 0, 0)  7.21 us
    pallas_call x1, Pallas kernels, local_norms(): pl.pallas_call(norms_kernel, grid=(MICRO,), in_specs=[pl.BlockSpec((1, RO...  5.32 us
    pallas_call x2, Pallas kernels, clipped_grad(): pl.pallas_call(functools.partial(grad_kernel, members), in_specs=[pl.Bloc...  5 us
    pallas_call x1, Pallas kernels, flip(): pl.pallas_call(flip_kernel, in_specs=[pl.BlockSpec(memory_space=pltpu.HBM...  4.07 us
    all_to_all x1, waiting for transfers between devices, body(): squares = lax.all_to_all(partial, ('y', 'core'), 0, 0)  3.4 us
  transfers between devices with their start and end apart: 4, of which 4 were waited for; matrix products, arithmetic and copies ran while one was open for 0% of the time, Pallas kernels for 8%

profile of v5, /device:TPU:6, one launch (start us, length us, event | category | flops | bytes accessed | tf_op | source)
XLA Modules:
  0.0 69.0 jit_solution(4149263861524106599)
XLA Ops:
  0.0 5.3 %norms.1 = f32[16,1,128]{2,1,0:T(1,128)} custom-call(bf16[2,768,512]{2,1,0:T(8,128)(2,1)} %x_hbm.3, bf16[2,768,1024]{2,1,0:T(8,128)(2,1)} %g_ref.1, s32[2,768]{1,0:T(2,128)} %u_hbm.3), custom_call_target="tpu_custom_call" | custom-call | tf_op jit(solution)/shard_map/norms/pallas_call | solution.py:63
  5.3 7.2 %all-to-all-start = ((f32[16,1,128]{2,1,0:T(1,128)}), f32[16,1,128]{2,1,0:T(1,128)S(1)}, u32[]{:S(2)}, u32[]{:S(2)}) async-start(f32[16,1,128]{2,1,0:T(1,128)} %norms.1), calls=%async_computation | async-start | bytes 16384 | tf_op jit(solution)/shard_map/all_to_all | solution.py:204
  12.5 0.0 copy-start.2
  12.5 4.1 %flip.1.gt_hbm = bf16[4,8,32,1536]{3,2,1,0:T(8,128)(2,1)} custom-call(bf16[2,768,1024]{2,1,0:T(8,128)(2,1)} %g_ref.1), custom_call_target="tpu_custom_call" | custom-call | tf_op jit(solution)/shard_map/flip/pallas_call | solution.py:114
  16.6 0.0 copy-start
  16.6 3.4 %all-to-all-done.sq_ref = f32[16,1,128]{2,1,0:T(1,128)S(1)} async-done(((f32[16,1,128]{2,1,0:T(1,128)}), f32[16,1,128]{2,1,0:T(1,128)S(1)}, u32[]{:S(2)}, u32[]{:S(2)}) %all-to-all-start) | async-done | bytes 8224 | tf_op jit(solution)/shard_map/all_to_all | solution.py:204
  20.0 0.0 copy-done.2
  20.0 0.0 copy-start.1
  20.0 3.7 %grad.3 = (f32[256,512]{1,0:T(8,128)S(1)}, f32[256,512]{1,0:T(8,128)S(1)}, f32[256,512]{1,0:T(8,128)S(1)}) custom-call(bf16[4,8,32,1536]{3,2,1,0:T(8,128)(2,1)} %flip.1.gt_hbm, bf16[2,768,512]{2,1,0:T(8,128)(2,1)} %x_hbm.3, s32[2,768]{1,0:T(2,128)S(1)} %copy-done.2, f32[16,1,128]{2,1,0:T(1,128)S(1)} %all-to-all-done.sq_ref), custom_call_target="tpu_custom_call" | custom-call | tf_op jit(solution)/shard_map/grad/pallas_call | solution.py:168
  23.7 4.5 %collective-permute-start = (f32[256,512]{1,0:T(8,128)S(1)}, f32[256,512]{1,0:T(8,128)S(1)}, u32[]{:S(2)}, u32[]{:S(2)}) collective-permute-start(f32[256,512]{1,0:T(8,128)S(1)} %get-tuple-element.8), channel_id=1, source_target_pairs={{0,80},{16,64},{32,112},{48,96},{64,16},{80,0},{96,48},{112,32},{1... | collective-permute-start | bytes 1572872 | tf_op jit(solution)/shard_map/ppermute | solution.py:210
  28.3 3.1 %collective-permute-start.1 = (f32[256,512]{1,0:T(8,128)S(1)}, f32[256,512]{1,0:T(8,128)S(1)}, u32[]{:S(2)}, u32[]{:S(2)}) collective-permute-start(f32[256,512]{1,0:T(8,128)S(1)} %get-tuple-element.9), channel_id=1, source_target_pairs={{0,16},{16,0},{32,48},{48,32},{64,80},{80,64},{96,112},{112,96},{1... | collective-permute-start | bytes 1572872 | tf_op jit(solution)/shard_map/ppermute | solution.py:210
  31.4 1.9 %collective-permute-start.2 = (f32[256,512]{1,0:T(8,128)S(1)}, f32[256,512]{1,0:T(8,128)S(1)}, u32[]{:S(2)}, u32[]{:S(2)}) collective-permute-start(f32[256,512]{1,0:T(8,128)S(1)} %get-tuple-element.10), channel_id=1, source_target_pairs={{0,64},{16,80},{32,96},{48,112},{64,0},{80,16},{96,32},{112,48},{1... | collective-permute-start | bytes 1572872 | tf_op jit(solution)/shard_map/ppermute | solution.py:210
  33.3 0.0 copy-done
  33.3 0.0 copy-done.1
  33.3 1.3 %grad.2 = f32[256,512]{1,0:T(8,128)S(1)} custom-call(bf16[4,8,32,1536]{3,2,1,0:T(8,128)(2,1)S(1)} %copy-done, bf16[2,768,512]{2,1,0:T(8,128)(2,1)S(1)} %copy-done.1, s32[2,768]{1,0:T(2,128)S(1)} %copy-done.2, f32[16,1,128]{2,1,0:T(1,128)S(1)} %all-to-all-done.sq_ref), custom_call_target="tpu_custom_call" | custom-call | tf_op jit(solution)/shard_map/grad/pallas_call | solution.py:168
  34.7 1.1 %collective-permute-done = f32[256,512]{1,0:T(8,128)S(1)} collective-permute-done((f32[256,512]{1,0:T(8,128)S(1)}, f32[256,512]{1,0:T(8,128)S(1)}, u32[]{:S(2)}, u32[]{:S(2)}) %collective-permute-start) | collective-permute-done | bytes 524320 | tf_op jit(solution)/shard_map/ppermute | solution.py:210
  35.8 5.5 %collective-permute-done.1 = f32[256,512]{1,0:T(8,128)S(1)} collective-permute-done((f32[256,512]{1,0:T(8,128)S(1)}, f32[256,512]{1,0:T(8,128)S(1)}, u32[]{:S(2)}, u32[]{:S(2)}) %collective-permute-start.1) | collective-permute-done | bytes 524320 | tf_op jit(solution)/shard_map/ppermute | solution.py:210
  41.3 1.1 %collective-permute-done.2 = f32[256,512]{1,0:T(8,128)S(1)} collective-permute-done((f32[256,512]{1,0:T(8,128)S(1)}, f32[256,512]{1,0:T(8,128)S(1)}, u32[]{:S(2)}, u32[]{:S(2)}) %collective-permute-start.2) | collective-permute-done | bytes 524320 | tf_op jit(solution)/shard_map/ppermute | solution.py:210
  42.5 0.2 add_add_fusion
  42.7 25.7 %all_to_all.10 = f32[8,32,512]{2,1,0:T(8,128)S(1)} all-to-all(f32[8,32,512]{2,1,0:T(8,128)S(1)} %bitcast.1), channel_id=1, replica_groups={{0,48,128,176,320,368,448,496},{16,32,144,160,336,352,464,480},{64,112,..., dimensions={0} | all-to-all | bytes 1048576 | tf_op jit(solution)/shard_map/all_to_all | solution.py:213
  68.4 0.7 reduce_sum.9
Async XLA Ops:
  5.3 14.7 %all-to-all-start = ((f32[16,1,128]{2,1,0:T(1,128)}), f32[16,1,128]{2,1,0:T(1,128)S(1)}, u32[]{:S(2)}, u32[]{:S(2)}) async-start(f32[16,1,128]{2,1,0:T(1,128)} %norms.1), calls=%async_computation | async-start | bytes 16384 | tf_op jit(solution)/shard_map/all_to_all | solution.py:204
  12.5 7.5 %copy-start.2 = (s32[2,768]{1,0:T(2,128)S(1)}, s32[2,768]{1,0:T(2,128)}, u32[]{:S(2)}) copy-start(s32[2,768]{1,0:T(2,128)} %u_hbm.3) | copy-start | bytes 18436
  16.6 16.7 %copy-start = (bf16[4,8,32,1536]{3,2,1,0:T(8,128)(2,1)S(1)}, bf16[4,8,32,1536]{3,2,1,0:T(8,128)(2,1)}, u32[]{:S(2)}) copy-start(bf16[4,8,32,1536]{3,2,1,0:T(8,128)(2,1)} %flip.1.gt_hbm) | copy-start | bytes 9437188
  20.0 13.3 %copy-start.1 = (bf16[2,768,512]{2,1,0:T(8,128)(2,1)S(1)}, bf16[2,768,512]{2,1,0:T(8,128)(2,1)}, u32[]{:S(2)}) copy-start(bf16[2,768,512]{2,1,0:T(8,128)(2,1)} %x_hbm.3) | copy-start | bytes 4718596
  23.7 12.1 %collective-permute-start = (f32[256,512]{1,0:T(8,128)S(1)}, f32[256,512]{1,0:T(8,128)S(1)}, u32[]{:S(2)}, u32[]{:S(2)}) collective-permute-start(f32[256,512]{1,0:T(8,128)S(1)} %get-tuple-element.8), channel_id=1, source_target_pairs={{0,80},{16,64},{32,112},{48,96},{64,16},{80,0},{96,48},{112,32},{1... | collective-permute-start | bytes 1572872 | tf_op jit(solution)/shard_map/ppermute | solution.py:210
  28.3 13.0 %collective-permute-start.1 = (f32[256,512]{1,0:T(8,128)S(1)}, f32[256,512]{1,0:T(8,128)S(1)}, u32[]{:S(2)}, u32[]{:S(2)}) collective-permute-start(f32[256,512]{1,0:T(8,128)S(1)} %get-tuple-element.9), channel_id=1, source_target_pairs={{0,16},{16,0},{32,48},{48,32},{64,80},{80,64},{96,112},{112,96},{1... | collective-permute-start | bytes 1572872 | tf_op jit(solution)/shard_map/ppermute | solution.py:210
  31.4 11.1 %collective-permute-start.2 = (f32[256,512]{1,0:T(8,128)S(1)}, f32[256,512]{1,0:T(8,128)S(1)}, u32[]{:S(2)}, u32[]{:S(2)}) collective-permute-start(f32[256,512]{1,0:T(8,128)S(1)} %get-tuple-element.10), channel_id=1, source_target_pairs={{0,64},{16,80},{32,96},{48,112},{64,0},{80,16},{96,32},{112,48},{1... | collective-permute-start | bytes 1572872 | tf_op jit(solution)/shard_map/ppermute | solution.py:210

commit v6 on v5

--- a/solution.py
+++ b/solution.py
@@ -16,6 +16,8 @@
 NZ, NX, NY, NC = 8, 4, 8, 2
 NU, NT = NZ * NX, NY * NC
 SENT = (3, 1, 2)
+Z_SHIFT = (1, 6)
+X_SHIFT = (1, 0)
 Z_CLASSES = ((0, 2, 5, 7), (1, 3, 4, 6))
 X_CLASSES = ((0, 3), (1, 2))
 MEMBERS, DESTS = 4, 8
@@ -77,9 +79,11 @@
 
 def my_place():
     core = lax.axis_index("core")
-    zc = lax.rem(lax.axis_index("z") + NZ - core, NZ)
-    xc = lax.rem(lax.axis_index("x") + NX - core, NX)
-    return core, class_of(zc, xc)
+    z_shift = jnp.where(core == 0, Z_SHIFT[0], Z_SHIFT[1])
+    x_shift = jnp.where(core == 0, X_SHIFT[0], X_SHIFT[1])
+    zc = lax.rem(lax.axis_index("z") + NZ - z_shift, NZ)
+    xc = lax.rem(lax.axis_index("x") + NX - x_shift, NX)
+    return z_shift, x_shift, class_of(zc, xc)
 
 
 def class_of(zc, xc):
@@ -88,7 +92,7 @@
 
 
 def flip_kernel(g_hbm, out_hbm, g_ref, out_ref, sems):
-    core, own = my_place()
+    z_shift, x_shift, own = my_place()
     reads = [pltpu.make_async_copy(g_hbm.at[m], g_ref.at[m], sems.at[0, m]) for m in range(MICRO)]
     writes = [pltpu.make_async_copy(out_ref.at[k], out_hbm.at[k], sems.at[1, k]) for k in range(MEMBERS)]
     for copy in reads:
@@ -97,9 +101,9 @@
         reads[m].wait()
         for z in range(NZ):
             flipped = jnp.transpose(g_ref[m, :, z * NX * OUT:(z + 1) * NX * OUT])
-            zc = lax.rem(z + NZ - core, NZ)
+            zc = lax.rem(z + NZ - z_shift, NZ)
             for x in range(NX):
-                xc = lax.rem(x + NX - core, NX)
+                xc = lax.rem(x + NX - x_shift, NX)
                 member = lax.bitwise_xor(class_of(zc, xc), own)
                 dest = 2 * (zc // 2) + xc // 2
                 out_ref[member, dest, :, m * ROWS:(m + 1) * ROWS] = flipped[x * OUT:(x + 1) * OUT, :]
@@ -184,7 +188,7 @@
 
 
 def place(zc, xc, core):
-    return ((zc + core) % NZ * NX + (xc + core) % NX) * NC + core
+    return ((zc + Z_SHIFT[core]) % NZ * NX + (xc + X_SHIFT[core]) % NX) * NC + core
 
 
 def stage_groups():

time: 69.5 us -> 67.3 us (0.968)
  blocking collectives: 25.7 us -> 14.6 us
  starting transfers between devices: 16.8 us -> 24.7 us
  waiting for transfers between devices: 11.2 us -> 12.4 us
    all_to_all x1, blocking collectives: 25.7 us -> 14.6 us  [body(): lax.all_to_all(total, axes, 0, 0, axis_index_groups=second)]
    ppermute x3, starting transfers between devices: 9.57 us -> 17.5 us  [body(): got = [lax.ppermute(part, axes, first[k]) for k, part in zip(SENT, sent)]]
    ppermute x3, waiting for transfers between devices: 7.8 us -> 9 us  [body(): got = [lax.ppermute(part, axes, first[k]) for k, part in zip(SENT, sent)]]
  transfers between devices with their start and end apart: 4 -> 4, of which waited for: 4 -> 3; matrix products, arithmetic and copies ran while one was open for 0% -> 0% of each run, Pallas kernels for 8% -> 8%
where the time goes in v6:
time: 67.3 us; the launch traced here: 67 us
  starting transfers between devices  24.7 us (37%)
  blocking collectives  14.6 us (22%)
  Pallas kernels  14.4 us (21%)
  waiting for transfers between devices  12.4 us (18%)
  other arithmetic  0.88 us (1%)
    ppermute x3, starting transfers between devices, body(): got = [lax.ppermute(part, axes, first[k]) for k, part in zip(SENT, sent)]  17.5 us
    all_to_all x1, blocking collectives, body(): lax.all_to_all(total, axes, 0, 0, axis_index_groups=second)  14.6 us
    ppermute x3, waiting for transfers between devices, body(): got = [lax.ppermute(part, axes, first[k]) for k, part in zip(SENT, sent)]  9 us
    all_to_all x1, starting transfers between devices, body(): squares = lax.all_to_all(partial, ('y', 'core'), 0, 0)  7.21 us
    pallas_call x1, Pallas kernels, local_norms(): pl.pallas_call(norms_kernel, grid=(MICRO,), in_specs=[pl.BlockSpec((1, RO...  5.32 us
    pallas_call x2, Pallas kernels, clipped_grad(): pl.pallas_call(functools.partial(grad_kernel, members), in_specs=[pl.Bloc...  5 us
    pallas_call x1, Pallas kernels, flip(): pl.pallas_call(flip_kernel, in_specs=[pl.BlockSpec(memory_space=pltpu.HBM...  4.07 us
    all_to_all x1, waiting for transfers between devices, body(): squares = lax.all_to_all(partial, ('y', 'core'), 0, 0)  3.4 us
  transfers between devices with their start and end apart: 4, of which 3 were waited for; matrix products, arithmetic and copies ran while one was open for 0% of the time, Pallas kernels for 8%

profile of v6, /device:TPU:6, one launch (start us, length us, event | category | flops | bytes accessed | tf_op | source)
XLA Modules:
  0.0 67.0 jit_solution(15039462491384827656)
XLA Ops:
  0.0 5.3 %norms.1 = f32[16,1,128]{2,1,0:T(1,128)} custom-call(bf16[2,768,512]{2,1,0:T(8,128)(2,1)} %x_hbm.3, bf16[2,768,1024]{2,1,0:T(8,128)(2,1)} %g_ref.1, s32[2,768]{1,0:T(2,128)} %u_hbm.3), custom_call_target="tpu_custom_call" | custom-call | tf_op jit(solution)/shard_map/norms/pallas_call | solution.py:65
  5.3 7.2 %all-to-all-start = ((f32[16,1,128]{2,1,0:T(1,128)}), f32[16,1,128]{2,1,0:T(1,128)S(1)}, u32[]{:S(2)}, u32[]{:S(2)}) async-start(f32[16,1,128]{2,1,0:T(1,128)} %norms.1), calls=%async_computation | async-start | bytes 16384 | tf_op jit(solution)/shard_map/all_to_all | solution.py:208
  12.5 0.0 copy-start.2
  12.5 4.1 %flip.1.gt_hbm = bf16[4,8,32,1536]{3,2,1,0:T(8,128)(2,1)} custom-call(bf16[2,768,1024]{2,1,0:T(8,128)(2,1)} %g_ref.1), custom_call_target="tpu_custom_call" | custom-call | tf_op jit(solution)/shard_map/flip/pallas_call | solution.py:118
  16.6 0.0 copy-start
  16.6 3.4 %all-to-all-done.sq_ref = f32[16,1,128]{2,1,0:T(1,128)S(1)} async-done(((f32[16,1,128]{2,1,0:T(1,128)}), f32[16,1,128]{2,1,0:T(1,128)S(1)}, u32[]{:S(2)}, u32[]{:S(2)}) %all-to-all-start) | async-done | bytes 8224 | tf_op jit(solution)/shard_map/all_to_all | solution.py:208
  20.0 0.0 copy-done.2
  20.0 0.0 copy-start.1
  20.0 3.7 %grad.3 = (f32[256,512]{1,0:T(8,128)S(1)}, f32[256,512]{1,0:T(8,128)S(1)}, f32[256,512]{1,0:T(8,128)S(1)}) custom-call(bf16[4,8,32,1536]{3,2,1,0:T(8,128)(2,1)} %flip.1.gt_hbm, bf16[2,768,512]{2,1,0:T(8,128)(2,1)} %x_hbm.3, s32[2,768]{1,0:T(2,128)S(1)} %copy-done.2, f32[16,1,128]{2,1,0:T(1,128)S(1)} %all-to-all-done.sq_ref), custom_call_target="tpu_custom_call" | custom-call | tf_op jit(solution)/shard_map/grad/pallas_call | solution.py:172
  23.7 10.9 %collective-permute-start = (f32[256,512]{1,0:T(8,128)S(1)}, f32[256,512]{1,0:T(8,128)S(1)}, u32[]{:S(2)}, u32[]{:S(2)}) collective-permute-start(f32[256,512]{1,0:T(8,128)S(1)} %get-tuple-element.8), channel_id=1, source_target_pairs={{80,160},{96,144},{112,128},{64,176},{144,96},{160,80},{176,64},{1... | collective-permute-start | bytes 1572872 | tf_op jit(solution)/shard_map/ppermute | solution.py:214
  34.6 4.7 %collective-permute-start.1 = (f32[256,512]{1,0:T(8,128)S(1)}, f32[256,512]{1,0:T(8,128)S(1)}, u32[]{:S(2)}, u32[]{:S(2)}) collective-permute-start(f32[256,512]{1,0:T(8,128)S(1)} %get-tuple-element.9), channel_id=1, source_target_pairs={{80,96},{96,80},{112,64},{64,112},{144,160},{160,144},{176,128},{1... | collective-permute-start | bytes 1572872 | tf_op jit(solution)/shard_map/ppermute | solution.py:214
  39.3 1.9 %collective-permute-start.2 = (f32[256,512]{1,0:T(8,128)S(1)}, f32[256,512]{1,0:T(8,128)S(1)}, u32[]{:S(2)}, u32[]{:S(2)}) collective-permute-start(f32[256,512]{1,0:T(8,128)S(1)} %get-tuple-element.10), channel_id=1, source_target_pairs={{80,144},{96,160},{112,176},{64,128},{144,80},{160,96},{176,112},{... | collective-permute-start | bytes 1572872 | tf_op jit(solution)/shard_map/ppermute | solution.py:214
  41.2 0.0 copy-done
  41.2 0.0 copy-done.1
  41.2 1.3 %grad.2 = f32[256,512]{1,0:T(8,128)S(1)} custom-call(bf16[4,8,32,1536]{3,2,1,0:T(8,128)(2,1)S(1)} %copy-done, bf16[2,768,512]{2,1,0:T(8,128)(2,1)S(1)} %copy-done.1, s32[2,768]{1,0:T(2,128)S(1)} %copy-done.2, f32[16,1,128]{2,1,0:T(1,128)S(1)} %all-to-all-done.sq_ref), custom_call_target="tpu_custom_call" | custom-call | tf_op jit(solution)/shard_map/grad/pallas_call | solution.py:172
  42.6 0.0 collective-permute-done
  42.6 4.8 %collective-permute-done.1 = f32[256,512]{1,0:T(8,128)S(1)} collective-permute-done((f32[256,512]{1,0:T(8,128)S(1)}, f32[256,512]{1,0:T(8,128)S(1)}, u32[]{:S(2)}, u32[]{:S(2)}) %collective-permute-start.1) | collective-permute-done | bytes 524320 | tf_op jit(solution)/shard_map/ppermute | solution.py:214
  47.4 4.2 %collective-permute-done.2 = f32[256,512]{1,0:T(8,128)S(1)} collective-permute-done((f32[256,512]{1,0:T(8,128)S(1)}, f32[256,512]{1,0:T(8,128)S(1)}, u32[]{:S(2)}, u32[]{:S(2)}) %collective-permute-start.2) | collective-permute-done | bytes 524320 | tf_op jit(solution)/shard_map/ppermute | solution.py:214
  51.6 0.2 add_add_fusion
  51.8 14.6 %all_to_all.10 = f32[8,32,512]{2,1,0:T(8,128)S(1)} all-to-all(f32[8,32,512]{2,1,0:T(8,128)S(1)} %bitcast.1), channel_id=1, replica_groups={{80,64,208,192,400,384,16,0},{96,112,224,240,416,432,32,48},{144,128,27..., dimensions={0} | all-to-all | bytes 1048576 | tf_op jit(solution)/shard_map/all_to_all | solution.py:217
  66.4 0.7 reduce_sum.9
Async XLA Ops:
  5.3 14.7 %all-to-all-start = ((f32[16,1,128]{2,1,0:T(1,128)}), f32[16,1,128]{2,1,0:T(1,128)S(1)}, u32[]{:S(2)}, u32[]{:S(2)}) async-start(f32[16,1,128]{2,1,0:T(1,128)} %norms.1), calls=%async_computation | async-start | bytes 16384 | tf_op jit(solution)/shard_map/all_to_all | solution.py:208
  12.5 7.5 %copy-start.2 = (s32[2,768]{1,0:T(2,128)S(1)}, s32[2,768]{1,0:T(2,128)}, u32[]{:S(2)}) copy-start(s32[2,768]{1,0:T(2,128)} %u_hbm.3) | copy-start | bytes 18436
  16.6 24.6 %copy-start = (bf16[4,8,32,1536]{3,2,1,0:T(8,128)(2,1)S(1)}, bf16[4,8,32,1536]{3,2,1,0:T(8,128)(2,1)}, u32[]{:S(2)}) copy-start(bf16[4,8,32,1536]{3,2,1,0:T(8,128)(2,1)} %flip.1.gt_hbm) | copy-start | bytes 9437188
  20.0 21.2 %copy-start.1 = (bf16[2,768,512]{2,1,0:T(8,128)(2,1)S(1)}, bf16[2,768,512]{2,1,0:T(8,128)(2,1)}, u32[]{:S(2)}) copy-start(bf16[2,768,512]{2,1,0:T(8,128)(2,1)} %x_hbm.3) | copy-start | bytes 4718596
  23.7 18.8 %collective-permute-start = (f32[256,512]{1,0:T(8,128)S(1)}, f32[256,512]{1,0:T(8,128)S(1)}, u32[]{:S(2)}, u32[]{:S(2)}) collective-permute-start(f32[256,512]{1,0:T(8,128)S(1)} %get-tuple-element.8), channel_id=1, source_target_pairs={{80,160},{96,144},{112,128},{64,176},{144,96},{160,80},{176,64},{1... | collective-permute-start | bytes 1572872 | tf_op jit(solution)/shard_map/ppermute | solution.py:214
  34.6 12.8 %collective-permute-start.1 = (f32[256,512]{1,0:T(8,128)S(1)}, f32[256,512]{1,0:T(8,128)S(1)}, u32[]{:S(2)}, u32[]{:S(2)}) collective-permute-start(f32[256,512]{1,0:T(8,128)S(1)} %get-tuple-element.9), channel_id=1, source_target_pairs={{80,96},{96,80},{112,64},{64,112},{144,160},{160,144},{176,128},{1... | collective-permute-start | bytes 1572872 | tf_op jit(solution)/shard_map/ppermute | solution.py:214
  39.3 12.3 %collective-permute-start.2 = (f32[256,512]{1,0:T(8,128)S(1)}, f32[256,512]{1,0:T(8,128)S(1)}, u32[]{:S(2)}, u32[]{:S(2)}) collective-permute-start(f32[256,512]{1,0:T(8,128)S(1)} %get-tuple-element.10), channel_id=1, source_target_pairs={{80,144},{96,160},{112,176},{64,128},{144,80},{160,96},{176,112},{... | collective-permute-start | bytes 1572872 | tf_op jit(solution)/shard_map/ppermute | solution.py:214

commit v7 on v6

--- a/solution.py
+++ b/solution.py
@@ -105,7 +105,7 @@
             for x in range(NX):
                 xc = lax.rem(x + NX - x_shift, NX)
                 member = lax.bitwise_xor(class_of(zc, xc), own)
-                dest = 2 * (zc // 2) + xc // 2
+                dest = 2 * (lax.rem(zc // 2, 2) * 2 + zc // 4) + xc // 2
                 out_ref[member, dest, :, m * ROWS:(m + 1) * ROWS] = flipped[x * OUT:(x + 1) * OUT, :]
     for copy in writes:
         copy.start()
@@ -197,7 +197,7 @@
         for k in range(MEMBERS)
     ]
     second = [
-        [place(z, x, core) for z in along_z for x in along_x]
+        [place(z, x, core) for z in (along_z[i] for i in (0, 2, 1, 3)) for x in along_x]
         for core in range(NC) for along_z in Z_CLASSES for along_x in X_CLASSES
     ]
     return first, second

time: 67.3 us -> 67.2 us (level)
  blocking collectives: 14.6 us -> 13.9 us
where the time goes in v7:
time: 67.2 us; the launch traced here: 66.4 us
  starting transfers between devices  24.7 us (37%)
  Pallas kernels  14.4 us (21%)
  blocking collectives  13.9 us (21%)
  waiting for transfers between devices  12.4 us (18%)
  other arithmetic  0.88 us (1%)
    ppermute x3, starting transfers between devices, body(): got = [lax.ppermute(part, axes, first[k]) for k, part in zip(SENT, sent)]  17.5 us
    all_to_all x1, blocking collectives, body(): lax.all_to_all(total, axes, 0, 0, axis_index_groups=second)  13.9 us
    ppermute x3, waiting for transfers between devices, body(): got = [lax.ppermute(part, axes, first[k]) for k, part in zip(SENT, sent)]  9 us
    all_to_all x1, starting transfers between devices, body(): squares = lax.all_to_all(partial, ('y', 'core'), 0, 0)  7.21 us
    pallas_call x1, Pallas kernels, local_norms(): pl.pallas_call(norms_kernel, grid=(MICRO,), in_specs=[pl.BlockSpec((1, RO...  5.32 us
    pallas_call x2, Pallas kernels, clipped_grad(): pl.pallas_call(functools.partial(grad_kernel, members), in_specs=[pl.Bloc...  5 us
    pallas_call x1, Pallas kernels, flip(): pl.pallas_call(flip_kernel, in_specs=[pl.BlockSpec(memory_space=pltpu.HBM...  4.07 us
    all_to_all x1, waiting for transfers between devices, body(): squares = lax.all_to_all(partial, ('y', 'core'), 0, 0)  3.4 us
  transfers between devices with their start and end apart: 4, of which 3 were waited for; matrix products, arithmetic and copies ran while one was open for 0% of the time, Pallas kernels for 8%

profile of v7, /device:TPU:6, one launch (start us, length us, event | category | flops | bytes accessed | tf_op | source)
XLA Modules:
  0.0 66.4 jit_solution(7816669665673725795)
XLA Ops:
  0.0 5.3 %norms.1 = f32[16,1,128]{2,1,0:T(1,128)} custom-call(bf16[2,768,512]{2,1,0:T(8,128)(2,1)} %x_hbm.3, bf16[2,768,1024]{2,1,0:T(8,128)(2,1)} %g_ref.1, s32[2,768]{1,0:T(2,128)} %u_hbm.3), custom_call_target="tpu_custom_call" | custom-call | tf_op jit(solution)/shard_map/norms/pallas_call | solution.py:65
  5.3 7.2 %all-to-all-start = ((f32[16,1,128]{2,1,0:T(1,128)}), f32[16,1,128]{2,1,0:T(1,128)S(1)}, u32[]{:S(2)}, u32[]{:S(2)}) async-start(f32[16,1,128]{2,1,0:T(1,128)} %norms.1), calls=%async_computation | async-start | bytes 16384 | tf_op jit(solution)/shard_map/all_to_all | solution.py:208
  12.5 0.0 copy-start.2
  12.5 4.1 %flip.1.gt_hbm = bf16[4,8,32,1536]{3,2,1,0:T(8,128)(2,1)} custom-call(bf16[2,768,1024]{2,1,0:T(8,128)(2,1)} %g_ref.1), custom_call_target="tpu_custom_call" | custom-call | tf_op jit(solution)/shard_map/flip/pallas_call | solution.py:118
  16.6 0.0 copy-start
  16.6 3.4 %all-to-all-done.sq_ref = f32[16,1,128]{2,1,0:T(1,128)S(1)} async-done(((f32[16,1,128]{2,1,0:T(1,128)}), f32[16,1,128]{2,1,0:T(1,128)S(1)}, u32[]{:S(2)}, u32[]{:S(2)}) %all-to-all-start) | async-done | bytes 8224 | tf_op jit(solution)/shard_map/all_to_all | solution.py:208
  20.0 0.0 copy-done.2
  20.0 0.0 copy-start.1
  20.0 3.7 %grad.3 = (f32[256,512]{1,0:T(8,128)S(1)}, f32[256,512]{1,0:T(8,128)S(1)}, f32[256,512]{1,0:T(8,128)S(1)}) custom-call(bf16[4,8,32,1536]{3,2,1,0:T(8,128)(2,1)} %flip.1.gt_hbm, bf16[2,768,512]{2,1,0:T(8,128)(2,1)} %x_hbm.3, s32[2,768]{1,0:T(2,128)S(1)} %copy-done.2, f32[16,1,128]{2,1,0:T(1,128)S(1)} %all-to-all-done.sq_ref), custom_call_target="tpu_custom_call" | custom-call | tf_op jit(solution)/shard_map/grad/pallas_call | solution.py:172
  23.7 10.9 %collective-permute-start = (f32[256,512]{1,0:T(8,128)S(1)}, f32[256,512]{1,0:T(8,128)S(1)}, u32[]{:S(2)}, u32[]{:S(2)}) collective-permute-start(f32[256,512]{1,0:T(8,128)S(1)} %get-tuple-element.8), channel_id=1, source_target_pairs={{80,160},{96,144},{112,128},{64,176},{144,96},{160,80},{176,64},{1... | collective-permute-start | bytes 1572872 | tf_op jit(solution)/shard_map/ppermute | solution.py:214
  34.6 4.7 %collective-permute-start.1 = (f32[256,512]{1,0:T(8,128)S(1)}, f32[256,512]{1,0:T(8,128)S(1)}, u32[]{:S(2)}, u32[]{:S(2)}) collective-permute-start(f32[256,512]{1,0:T(8,128)S(1)} %get-tuple-element.9), channel_id=1, source_target_pairs={{80,96},{96,80},{112,64},{64,112},{144,160},{160,144},{176,128},{1... | collective-permute-start | bytes 1572872 | tf_op jit(solution)/shard_map/ppermute | solution.py:214
  39.3 1.9 %collective-permute-start.2 = (f32[256,512]{1,0:T(8,128)S(1)}, f32[256,512]{1,0:T(8,128)S(1)}, u32[]{:S(2)}, u32[]{:S(2)}) collective-permute-start(f32[256,512]{1,0:T(8,128)S(1)} %get-tuple-element.10), channel_id=1, source_target_pairs={{80,144},{96,160},{112,176},{64,128},{144,80},{160,96},{176,112},{... | collective-permute-start | bytes 1572872 | tf_op jit(solution)/shard_map/ppermute | solution.py:214
  41.2 0.0 copy-done
  41.2 0.0 copy-done.1
  41.2 1.3 %grad.2 = f32[256,512]{1,0:T(8,128)S(1)} custom-call(bf16[4,8,32,1536]{3,2,1,0:T(8,128)(2,1)S(1)} %copy-done, bf16[2,768,512]{2,1,0:T(8,128)(2,1)S(1)} %copy-done.1, s32[2,768]{1,0:T(2,128)S(1)} %copy-done.2, f32[16,1,128]{2,1,0:T(1,128)S(1)} %all-to-all-done.sq_ref), custom_call_target="tpu_custom_call" | custom-call | tf_op jit(solution)/shard_map/grad/pallas_call | solution.py:172
  42.6 0.0 collective-permute-done
  42.6 4.8 %collective-permute-done.1 = f32[256,512]{1,0:T(8,128)S(1)} collective-permute-done((f32[256,512]{1,0:T(8,128)S(1)}, f32[256,512]{1,0:T(8,128)S(1)}, u32[]{:S(2)}, u32[]{:S(2)}) %collective-permute-start.1) | collective-permute-done | bytes 524320 | tf_op jit(solution)/shard_map/ppermute | solution.py:214
  47.4 4.2 %collective-permute-done.2 = f32[256,512]{1,0:T(8,128)S(1)} collective-permute-done((f32[256,512]{1,0:T(8,128)S(1)}, f32[256,512]{1,0:T(8,128)S(1)}, u32[]{:S(2)}, u32[]{:S(2)}) %collective-permute-start.2) | collective-permute-done | bytes 524320 | tf_op jit(solution)/shard_map/ppermute | solution.py:214
  51.6 0.2 add_add_fusion
  51.8 13.9 %all_to_all.10 = f32[8,32,512]{2,1,0:T(8,128)S(1)} all-to-all(f32[8,32,512]{2,1,0:T(8,128)S(1)} %bitcast.1), channel_id=1, replica_groups={{80,64,400,384,208,192,16,0},{96,112,416,432,224,240,32,48},{144,128,33..., dimensions={0} | all-to-all | bytes 1048576 | tf_op jit(solution)/shard_map/all_to_all | solution.py:217
  65.7 0.7 %reduce_sum.9 = f32[32,512]{1,0:T(8,128)} reduce(f32[8,32,512]{2,1,0:T(8,128)S(1)} %all_to_all.10, f32[]{:T(128)} %constant.0.clone.1), dimensions={0}, to_apply=%region_0.0 | reduce | flops 114688 | bytes 589828 | tf_op jit(solution)/shard_map/reduce_sum | solution.py:217
Async XLA Ops:
  5.3 14.7 %all-to-all-start = ((f32[16,1,128]{2,1,0:T(1,128)}), f32[16,1,128]{2,1,0:T(1,128)S(1)}, u32[]{:S(2)}, u32[]{:S(2)}) async-start(f32[16,1,128]{2,1,0:T(1,128)} %norms.1), calls=%async_computation | async-start | bytes 16384 | tf_op jit(solution)/shard_map/all_to_all | solution.py:208
  12.5 7.5 %copy-start.2 = (s32[2,768]{1,0:T(2,128)S(1)}, s32[2,768]{1,0:T(2,128)}, u32[]{:S(2)}) copy-start(s32[2,768]{1,0:T(2,128)} %u_hbm.3) | copy-start | bytes 18436
  16.6 24.6 %copy-start = (bf16[4,8,32,1536]{3,2,1,0:T(8,128)(2,1)S(1)}, bf16[4,8,32,1536]{3,2,1,0:T(8,128)(2,1)}, u32[]{:S(2)}) copy-start(bf16[4,8,32,1536]{3,2,1,0:T(8,128)(2,1)} %flip.1.gt_hbm) | copy-start | bytes 9437188
  20.0 21.2 %copy-start.1 = (bf16[2,768,512]{2,1,0:T(8,128)(2,1)S(1)}, bf16[2,768,512]{2,1,0:T(8,128)(2,1)}, u32[]{:S(2)}) copy-start(bf16[2,768,512]{2,1,0:T(8,128)(2,1)} %x_hbm.3) | copy-start | bytes 4718596
  23.7 18.8 %collective-permute-start = (f32[256,512]{1,0:T(8,128)S(1)}, f32[256,512]{1,0:T(8,128)S(1)}, u32[]{:S(2)}, u32[]{:S(2)}) collective-permute-start(f32[256,512]{1,0:T(8,128)S(1)} %get-tuple-element.8), channel_id=1, source_target_pairs={{80,160},{96,144},{112,128},{64,176},{144,96},{160,80},{176,64},{1... | collective-permute-start | bytes 1572872 | tf_op jit(solution)/shard_map/ppermute | solution.py:214
  34.6 12.8 %collective-permute-start.1 = (f32[256,512]{1,0:T(8,128)S(1)}, f32[256,512]{1,0:T(8,128)S(1)}, u32[]{:S(2)}, u32[]{:S(2)}) collective-permute-start(f32[256,512]{1,0:T(8,128)S(1)} %get-tuple-element.9), channel_id=1, source_target_pairs={{80,96},{96,80},{112,64},{64,112},{144,160},{160,144},{176,128},{1... | collective-permute-start | bytes 1572872 | tf_op jit(solution)/shard_map/ppermute | solution.py:214
  39.3 12.3 %collective-permute-start.2 = (f32[256,512]{1,0:T(8,128)S(1)}, f32[256,512]{1,0:T(8,128)S(1)}, u32[]{:S(2)}, u32[]{:S(2)}) collective-permute-start(f32[256,512]{1,0:T(8,128)S(1)} %get-tuple-element.10), channel_id=1, source_target_pairs={{80,144},{96,160},{112,176},{64,128},{144,80},{160,96},{176,112},{... | collective-permute-start | bytes 1572872 | tf_op jit(solution)/shard_map/ppermute | solution.py:214

commit v8 on v7

--- a/solution.py
+++ b/solution.py
@@ -15,7 +15,7 @@
 USERS_MB = 8
 NZ, NX, NY, NC = 8, 4, 8, 2
 NU, NT = NZ * NX, NY * NC
-SENT = (3, 1, 2)
+SENT = (3, 2, 1)
 Z_SHIFT = (1, 6)
 X_SHIFT = (1, 0)
 Z_CLASSES = ((0, 2, 5, 7), (1, 3, 4, 6))
@@ -105,7 +105,7 @@
             for x in range(NX):
                 xc = lax.rem(x + NX - x_shift, NX)
                 member = lax.bitwise_xor(class_of(zc, xc), own)
-                dest = 2 * (lax.rem(zc // 2, 2) * 2 + zc // 4) + xc // 2
+                dest = zc // 2 + 4 * (xc // 2)
                 out_ref[member, dest, :, m * ROWS:(m + 1) * ROWS] = flipped[x * OUT:(x + 1) * OUT, :]
     for copy in writes:
         copy.start()
@@ -197,7 +197,7 @@
         for k in range(MEMBERS)
     ]
     second = [
-        [place(z, x, core) for z in (along_z[i] for i in (0, 2, 1, 3)) for x in along_x]
+        [place(z, x, core) for x in along_x for z in along_z]
         for core in range(NC) for along_z in Z_CLASSES for along_x in X_CLASSES
     ]
     return first, second

time: 67.2 us -> 66.3 us (0.987)
  waiting for transfers between devices: 12.4 us -> 9.74 us
  blocking collectives: 13.9 us -> 16.1 us
    ppermute x3, waiting for transfers between devices: 9 us -> 6.34 us  [body(): got = [lax.ppermute(part, axes, first[k]) for k, part in zip(SENT, sent)]]
    all_to_all x1, blocking collectives: 13.9 us -> 16.1 us  [body(): lax.all_to_all(total, axes, 0, 0, axis_index_groups=second)]
where the time goes in v8:
time: 66.3 us; the launch traced here: 65.9 us
  starting transfers between devices  24.7 us (37%)
  blocking collectives  16.1 us (24%)
  Pallas kernels  14.4 us (22%)
  waiting for transfers between devices  9.74 us (15%)
  other arithmetic  0.88 us (1%)
    ppermute x3, starting transfers between devices, body(): got = [lax.ppermute(part, axes, first[k]) for k, part in zip(SENT, sent)]  17.5 us
    all_to_all x1, blocking collectives, body(): lax.all_to_all(total, axes, 0, 0, axis_index_groups=second)  16.1 us
    all_to_all x1, starting transfers between devices, body(): squares = lax.all_to_all(partial, ('y', 'core'), 0, 0)  7.21 us
    ppermute x3, waiting for transfers between devices, body(): got = [lax.ppermute(part, axes, first[k]) for k, part in zip(SENT, sent)]  6.34 us
    pallas_call x1, Pallas kernels, local_norms(): pl.pallas_call(norms_kernel, grid=(MICRO,), in_specs=[pl.BlockSpec((1, RO...  5.32 us
    pallas_call x2, Pallas kernels, clipped_grad(): pl.pallas_call(functools.partial(grad_kernel, members), in_specs=[pl.Bloc...  5 us
    pallas_call x1, Pallas kernels, flip(): pl.pallas_call(flip_kernel, in_specs=[pl.BlockSpec(memory_space=pltpu.HBM...  4.07 us
    all_to_all x1, waiting for transfers between devices, body(): squares = lax.all_to_all(partial, ('y', 'core'), 0, 0)  3.4 us
  transfers between devices with their start and end apart: 4, of which 3 were waited for; matrix products, arithmetic and copies ran while one was open for 0% of the time, Pallas kernels for 8%

profile of v8, /device:TPU:6, one launch (start us, length us, event | category | flops | bytes accessed | tf_op | source)
XLA Modules:
  0.0 65.9 jit_solution(16543578998403498333)
XLA Ops:
  0.0 5.3 %norms.1 = f32[16,1,128]{2,1,0:T(1,128)} custom-call(bf16[2,768,512]{2,1,0:T(8,128)(2,1)} %x_hbm.3, bf16[2,768,1024]{2,1,0:T(8,128)(2,1)} %g_ref.1, s32[2,768]{1,0:T(2,128)} %u_hbm.3), custom_call_target="tpu_custom_call" | custom-call | tf_op jit(solution)/shard_map/norms/pallas_call | solution.py:65
  5.3 7.2 %all-to-all-start = ((f32[16,1,128]{2,1,0:T(1,128)}), f32[16,1,128]{2,1,0:T(1,128)S(1)}, u32[]{:S(2)}, u32[]{:S(2)}) async-start(f32[16,1,128]{2,1,0:T(1,128)} %norms.1), calls=%async_computation | async-start | bytes 16384 | tf_op jit(solution)/shard_map/all_to_all | solution.py:208
  12.5 0.0 copy-start.2
  12.5 4.1 %flip.1.gt_hbm = bf16[4,8,32,1536]{3,2,1,0:T(8,128)(2,1)} custom-call(bf16[2,768,1024]{2,1,0:T(8,128)(2,1)} %g_ref.1), custom_call_target="tpu_custom_call" | custom-call | tf_op jit(solution)/shard_map/flip/pallas_call | solution.py:118
  16.6 0.0 copy-start
  16.6 3.4 %all-to-all-done.sq_ref = f32[16,1,128]{2,1,0:T(1,128)S(1)} async-done(((f32[16,1,128]{2,1,0:T(1,128)}), f32[16,1,128]{2,1,0:T(1,128)S(1)}, u32[]{:S(2)}, u32[]{:S(2)}) %all-to-all-start) | async-done | bytes 8224 | tf_op jit(solution)/shard_map/all_to_all | solution.py:208
  20.0 0.0 copy-done.2
  20.0 0.0 copy-start.1
  20.0 3.7 %grad.3 = (f32[256,512]{1,0:T(8,128)S(1)}, f32[256,512]{1,0:T(8,128)S(1)}, f32[256,512]{1,0:T(8,128)S(1)}) custom-call(bf16[4,8,32,1536]{3,2,1,0:T(8,128)(2,1)} %flip.1.gt_hbm, bf16[2,768,512]{2,1,0:T(8,128)(2,1)} %x_hbm.3, s32[2,768]{1,0:T(2,128)S(1)} %copy-done.2, f32[16,1,128]{2,1,0:T(1,128)S(1)} %all-to-all-done.sq_ref), custom_call_target="tpu_custom_call" | custom-call | tf_op jit(solution)/shard_map/grad/pallas_call | solution.py:172
  23.7 10.9 %collective-permute-start = (f32[256,512]{1,0:T(8,128)S(1)}, f32[256,512]{1,0:T(8,128)S(1)}, u32[]{:S(2)}, u32[]{:S(2)}) collective-permute-start(f32[256,512]{1,0:T(8,128)S(1)} %get-tuple-element.8), channel_id=1, source_target_pairs={{80,160},{96,144},{112,128},{64,176},{144,96},{160,80},{176,64},{1... | collective-permute-start | bytes 1572872 | tf_op jit(solution)/shard_map/ppermute | solution.py:214
  34.6 2.0 %collective-permute-start.1 = (f32[256,512]{1,0:T(8,128)S(1)}, f32[256,512]{1,0:T(8,128)S(1)}, u32[]{:S(2)}, u32[]{:S(2)}) collective-permute-start(f32[256,512]{1,0:T(8,128)S(1)} %get-tuple-element.9), channel_id=1, source_target_pairs={{80,144},{96,160},{112,176},{64,128},{144,80},{160,96},{176,112},{... | collective-permute-start | bytes 1572872 | tf_op jit(solution)/shard_map/ppermute | solution.py:214
  36.6 4.6 %collective-permute-start.2 = (f32[256,512]{1,0:T(8,128)S(1)}, f32[256,512]{1,0:T(8,128)S(1)}, u32[]{:S(2)}, u32[]{:S(2)}) collective-permute-start(f32[256,512]{1,0:T(8,128)S(1)} %get-tuple-element.10), channel_id=1, source_target_pairs={{80,96},{96,80},{112,64},{64,112},{144,160},{160,144},{176,128},{1... | collective-permute-start | bytes 1572872 | tf_op jit(solution)/shard_map/ppermute | solution.py:214
  41.2 0.0 copy-done
  41.2 0.0 copy-done.1
  41.2 1.3 %grad.2 = f32[256,512]{1,0:T(8,128)S(1)} custom-call(bf16[4,8,32,1536]{3,2,1,0:T(8,128)(2,1)S(1)} %copy-done, bf16[2,768,512]{2,1,0:T(8,128)(2,1)S(1)} %copy-done.1, s32[2,768]{1,0:T(2,128)S(1)} %copy-done.2, f32[16,1,128]{2,1,0:T(1,128)S(1)} %all-to-all-done.sq_ref), custom_call_target="tpu_custom_call" | custom-call | tf_op jit(solution)/shard_map/grad/pallas_call | solution.py:172
  42.6 0.0 collective-permute-done
  42.6 4.9 %collective-permute-done.1 = f32[256,512]{1,0:T(8,128)S(1)} collective-permute-done((f32[256,512]{1,0:T(8,128)S(1)}, f32[256,512]{1,0:T(8,128)S(1)}, u32[]{:S(2)}, u32[]{:S(2)}) %collective-permute-start.1) | collective-permute-done | bytes 524320 | tf_op jit(solution)/shard_map/ppermute | solution.py:214
  47.5 1.5 %collective-permute-done.2 = f32[256,512]{1,0:T(8,128)S(1)} collective-permute-done((f32[256,512]{1,0:T(8,128)S(1)}, f32[256,512]{1,0:T(8,128)S(1)}, u32[]{:S(2)}, u32[]{:S(2)}) %collective-permute-start.2) | collective-permute-done | bytes 524320 | tf_op jit(solution)/shard_map/ppermute | solution.py:214
  48.9 0.2 add_add_fusion
  49.1 16.1 %all_to_all.10 = f32[8,32,512]{2,1,0:T(8,128)S(1)} all-to-all(f32[8,32,512]{2,1,0:T(8,128)S(1)} %bitcast.1), channel_id=1, replica_groups={{80,208,400,16,64,192,384,0},{96,224,416,32,112,240,432,48},{144,272,33..., dimensions={0} | all-to-all | bytes 1048576 | tf_op jit(solution)/shard_map/all_to_all | solution.py:217
  65.2 0.7 %reduce_sum.9 = f32[32,512]{1,0:T(8,128)} reduce(f32[8,32,512]{2,1,0:T(8,128)S(1)} %all_to_all.10, f32[]{:T(128)} %constant.0.clone.1), dimensions={0}, to_apply=%region_0.0 | reduce | flops 114688 | bytes 589828 | tf_op jit(solution)/shard_map/reduce_sum | solution.py:217
Async XLA Ops:
  5.3 14.7 %all-to-all-start = ((f32[16,1,128]{2,1,0:T(1,128)}), f32[16,1,128]{2,1,0:T(1,128)S(1)}, u32[]{:S(2)}, u32[]{:S(2)}) async-start(f32[16,1,128]{2,1,0:T(1,128)} %norms.1), calls=%async_computation | async-start | bytes 16384 | tf_op jit(solution)/shard_map/all_to_all | solution.py:208
  12.5 7.5 %copy-start.2 = (s32[2,768]{1,0:T(2,128)S(1)}, s32[2,768]{1,0:T(2,128)}, u32[]{:S(2)}) copy-start(s32[2,768]{1,0:T(2,128)} %u_hbm.3) | copy-start | bytes 18436
  16.6 24.6 %copy-start = (bf16[4,8,32,1536]{3,2,1,0:T(8,128)(2,1)S(1)}, bf16[4,8,32,1536]{3,2,1,0:T(8,128)(2,1)}, u32[]{:S(2)}) copy-start(bf16[4,8,32,1536]{3,2,1,0:T(8,128)(2,1)} %flip.1.gt_hbm) | copy-start | bytes 9437188
  20.0 21.2 %copy-start.1 = (bf16[2,768,512]{2,1,0:T(8,128)(2,1)S(1)}, bf16[2,768,512]{2,1,0:T(8,128)(2,1)}, u32[]{:S(2)}) copy-start(bf16[2,768,512]{2,1,0:T(8,128)(2,1)} %x_hbm.3) | copy-start | bytes 4718596
  23.7 18.8 %collective-permute-start = (f32[256,512]{1,0:T(8,128)S(1)}, f32[256,512]{1,0:T(8,128)S(1)}, u32[]{:S(2)}, u32[]{:S(2)}) collective-permute-start(f32[256,512]{1,0:T(8,128)S(1)} %get-tuple-element.8), channel_id=1, source_target_pairs={{80,160},{96,144},{112,128},{64,176},{144,96},{160,80},{176,64},{1... | collective-permute-start | bytes 1572872 | tf_op jit(solution)/shard_map/ppermute | solution.py:214
  34.6 12.9 %collective-permute-start.1 = (f32[256,512]{1,0:T(8,128)S(1)}, f32[256,512]{1,0:T(8,128)S(1)}, u32[]{:S(2)}, u32[]{:S(2)}) collective-permute-start(f32[256,512]{1,0:T(8,128)S(1)} %get-tuple-element.9), channel_id=1, source_target_pairs={{80,144},{96,160},{112,176},{64,128},{144,80},{160,96},{176,112},{... | collective-permute-start | bytes 1572872 | tf_op jit(solution)/shard_map/ppermute | solution.py:214
  36.6 12.3 %collective-permute-start.2 = (f32[256,512]{1,0:T(8,128)S(1)}, f32[256,512]{1,0:T(8,128)S(1)}, u32[]{:S(2)}, u32[]{:S(2)}) collective-permute-start(f32[256,512]{1,0:T(8,128)S(1)} %get-tuple-element.10), channel_id=1, source_target_pairs={{80,96},{96,80},{112,64},{64,112},{144,160},{160,144},{176,128},{1... | collective-permute-start | bytes 1572872 | tf_op jit(solution)/shard_map/ppermute | solution.py:214

commit v9 on v8

--- a/solution.py
+++ b/solution.py
@@ -105,7 +105,7 @@
             for x in range(NX):
                 xc = lax.rem(x + NX - x_shift, NX)
                 member = lax.bitwise_xor(class_of(zc, xc), own)
-                dest = zc // 2 + 4 * (xc // 2)
+                dest = lax.rem(zc // 2, 2) * 2 + zc // 4 + 4 * (xc // 2)
                 out_ref[member, dest, :, m * ROWS:(m + 1) * ROWS] = flipped[x * OUT:(x + 1) * OUT, :]
     for copy in writes:
         copy.start()
@@ -197,7 +197,7 @@
         for k in range(MEMBERS)
     ]
     second = [
-        [place(z, x, core) for x in along_x for z in along_z]
+        [place(z, x, core) for x in along_x for z in (along_z[i] for i in (0, 2, 1, 3))]
         for core in range(NC) for along_z in Z_CLASSES for along_x in X_CLASSES
     ]
     return first, second

time: 66.3 us -> 67.6 us (1.020)
  the two profiles are of different devices: /device:TPU:6 before, /device:TPU:8 now
where the time goes in v9:
time: 67.6 us; the launch traced here: 67.3 us
  starting transfers between devices  25 us (37%)
  blocking collectives  16.4 us (24%)
  Pallas kernels  14.4 us (21%)
  waiting for transfers between devices  10.5 us (16%)
  other arithmetic  0.88 us (1%)
    all_to_all x1, blocking collectives, body(): lax.all_to_all(total, axes, 0, 0, axis_index_groups=second)  16.4 us
    ppermute x3, starting transfers between devices, body(): got = [lax.ppermute(part, axes, first[k]) for k, part in zip(SENT, sent)]  16 us
    all_to_all x1, starting transfers between devices, body(): squares = lax.all_to_all(partial, ('y', 'core'), 0, 0)  9.09 us
    ppermute x3, waiting for transfers between devices, body(): got = [lax.ppermute(part, axes, first[k]) for k, part in zip(SENT, sent)]  8.46 us
    pallas_call x1, Pallas kernels, local_norms(): pl.pallas_call(norms_kernel, grid=(MICRO,), in_specs=[pl.BlockSpec((1, RO...  5.32 us
    pallas_call x2, Pallas kernels, clipped_grad(): pl.pallas_call(functools.partial(grad_kernel, members), in_specs=[pl.Bloc...  5 us
    pallas_call x1, Pallas kernels, flip(): pl.pallas_call(flip_kernel, in_specs=[pl.BlockSpec(memory_space=pltpu.HBM...  4.07 us
    all_to_all x1, waiting for transfers between devices, body(): squares = lax.all_to_all(partial, ('y', 'core'), 0, 0)  2.07 us
  transfers between devices with their start and end apart: 4, of which 4 were waited for; matrix products, arithmetic and copies ran while one was open for 0% of the time, Pallas kernels for 8%

profile of v9, /device:TPU:8, one launch (start us, length us, event | category | flops | bytes accessed | tf_op | source)
XLA Modules:
  0.0 67.3 jit_solution(2054921177326180600)
XLA Ops:
  0.0 5.3 %norms.1 = f32[16,1,128]{2,1,0:T(1,128)} custom-call(bf16[2,768,512]{2,1,0:T(8,128)(2,1)} %x_hbm.3, bf16[2,768,1024]{2,1,0:T(8,128)(2,1)} %g_ref.1, s32[2,768]{1,0:T(2,128)} %u_hbm.3), custom_call_target="tpu_custom_call" | custom-call | tf_op jit(solution)/shard_map/norms/pallas_call | solution.py:65
  5.3 9.1 %all-to-all-start = ((f32[16,1,128]{2,1,0:T(1,128)}), f32[16,1,128]{2,1,0:T(1,128)S(1)}, u32[]{:S(2)}, u32[]{:S(2)}) async-start(f32[16,1,128]{2,1,0:T(1,128)} %norms.1), calls=%async_computation | async-start | bytes 16384 | tf_op jit(solution)/shard_map/all_to_all | solution.py:208
  14.4 0.0 copy-start.2
  14.4 4.1 %flip.1.gt_hbm = bf16[4,8,32,1536]{3,2,1,0:T(8,128)(2,1)} custom-call(bf16[2,768,1024]{2,1,0:T(8,128)(2,1)} %g_ref.1), custom_call_target="tpu_custom_call" | custom-call | tf_op jit(solution)/shard_map/flip/pallas_call | solution.py:118
  18.5 0.0 copy-start
  18.5 2.1 %all-to-all-done.sq_ref = f32[16,1,128]{2,1,0:T(1,128)S(1)} async-done(((f32[16,1,128]{2,1,0:T(1,128)}), f32[16,1,128]{2,1,0:T(1,128)S(1)}, u32[]{:S(2)}, u32[]{:S(2)}) %all-to-all-start) | async-done | bytes 8224 | tf_op jit(solution)/shard_map/all_to_all | solution.py:208
  20.6 0.0 copy-done.2
  20.6 0.0 copy-start.1
  20.6 3.7 %grad.3 = (f32[256,512]{1,0:T(8,128)S(1)}, f32[256,512]{1,0:T(8,128)S(1)}, f32[256,512]{1,0:T(8,128)S(1)}) custom-call(bf16[4,8,32,1536]{3,2,1,0:T(8,128)(2,1)} %flip.1.gt_hbm, bf16[2,768,512]{2,1,0:T(8,128)(2,1)} %x_hbm.3, s32[2,768]{1,0:T(2,128)S(1)} %copy-done.2, f32[16,1,128]{2,1,0:T(1,128)S(1)} %all-to-all-done.sq_ref), custom_call_target="tpu_custom_call" | custom-call | tf_op jit(solution)/shard_map/grad/pallas_call | solution.py:172
  24.3 11.6 %collective-permute-start = (f32[256,512]{1,0:T(8,128)S(1)}, f32[256,512]{1,0:T(8,128)S(1)}, u32[]{:S(2)}, u32[]{:S(2)}) collective-permute-start(f32[256,512]{1,0:T(8,128)S(1)} %get-tuple-element.8), channel_id=1, source_target_pairs={{80,160},{96,144},{112,128},{64,176},{144,96},{160,80},{176,64},{1... | collective-permute-start | bytes 1572872 | tf_op jit(solution)/shard_map/ppermute | solution.py:214
  35.9 1.9 %collective-permute-start.1 = (f32[256,512]{1,0:T(8,128)S(1)}, f32[256,512]{1,0:T(8,128)S(1)}, u32[]{:S(2)}, u32[]{:S(2)}) collective-permute-start(f32[256,512]{1,0:T(8,128)S(1)} %get-tuple-element.9), channel_id=1, source_target_pairs={{80,144},{96,160},{112,176},{64,128},{144,80},{160,96},{176,112},{... | collective-permute-start | bytes 1572872 | tf_op jit(solution)/shard_map/ppermute | solution.py:214
  37.8 2.5 %collective-permute-start.2 = (f32[256,512]{1,0:T(8,128)S(1)}, f32[256,512]{1,0:T(8,128)S(1)}, u32[]{:S(2)}, u32[]{:S(2)}) collective-permute-start(f32[256,512]{1,0:T(8,128)S(1)} %get-tuple-element.10), channel_id=1, source_target_pairs={{80,96},{96,80},{112,64},{64,112},{144,160},{160,144},{176,128},{1... | collective-permute-start | bytes 1572872 | tf_op jit(solution)/shard_map/ppermute | solution.py:214
  40.3 0.0 copy-done
  40.3 0.0 copy-done.1
  40.3 1.3 %grad.2 = f32[256,512]{1,0:T(8,128)S(1)} custom-call(bf16[4,8,32,1536]{3,2,1,0:T(8,128)(2,1)S(1)} %copy-done, bf16[2,768,512]{2,1,0:T(8,128)(2,1)S(1)} %copy-done.1, s32[2,768]{1,0:T(2,128)S(1)} %copy-done.2, f32[16,1,128]{2,1,0:T(1,128)S(1)} %all-to-all-done.sq_ref), custom_call_target="tpu_custom_call" | custom-call | tf_op jit(solution)/shard_map/grad/pallas_call | solution.py:172
  41.6 1.4 %collective-permute-done = f32[256,512]{1,0:T(8,128)S(1)} collective-permute-done((f32[256,512]{1,0:T(8,128)S(1)}, f32[256,512]{1,0:T(8,128)S(1)}, u32[]{:S(2)}, u32[]{:S(2)}) %collective-permute-start) | collective-permute-done | bytes 524320 | tf_op jit(solution)/shard_map/ppermute | solution.py:214
  43.0 5.2 %collective-permute-done.1 = f32[256,512]{1,0:T(8,128)S(1)} collective-permute-done((f32[256,512]{1,0:T(8,128)S(1)}, f32[256,512]{1,0:T(8,128)S(1)}, u32[]{:S(2)}, u32[]{:S(2)}) %collective-permute-start.1) | collective-permute-done | bytes 524320 | tf_op jit(solution)/shard_map/ppermute | solution.py:214
  48.1 1.9 %collective-permute-done.2 = f32[256,512]{1,0:T(8,128)S(1)} collective-permute-done((f32[256,512]{1,0:T(8,128)S(1)}, f32[256,512]{1,0:T(8,128)S(1)}, u32[]{:S(2)}, u32[]{:S(2)}) %collective-permute-start.2) | collective-permute-done | bytes 524320 | tf_op jit(solution)/shard_map/ppermute | solution.py:214
  50.1 0.2 add_add_fusion
  50.3 16.4 %all_to_all.10 = f32[8,32,512]{2,1,0:T(8,128)S(1)} all-to-all(f32[8,32,512]{2,1,0:T(8,128)S(1)} %bitcast.1), channel_id=1, replica_groups={{80,400,208,16,64,384,192,0},{96,416,224,32,112,432,240,48},{144,336,27..., dimensions={0} | all-to-all | bytes 1048576 | tf_op jit(solution)/shard_map/all_to_all | solution.py:217
  66.6 0.7 reduce_sum.9
Async XLA Ops:
  5.3 15.3 %all-to-all-start = ((f32[16,1,128]{2,1,0:T(1,128)}), f32[16,1,128]{2,1,0:T(1,128)S(1)}, u32[]{:S(2)}, u32[]{:S(2)}) async-start(f32[16,1,128]{2,1,0:T(1,128)} %norms.1), calls=%async_computation | async-start | bytes 16384 | tf_op jit(solution)/shard_map/all_to_all | solution.py:208
  14.4 6.2 %copy-start.2 = (s32[2,768]{1,0:T(2,128)S(1)}, s32[2,768]{1,0:T(2,128)}, u32[]{:S(2)}) copy-start(s32[2,768]{1,0:T(2,128)} %u_hbm.3) | copy-start | bytes 18436
  18.5 21.8 %copy-start = (bf16[4,8,32,1536]{3,2,1,0:T(8,128)(2,1)S(1)}, bf16[4,8,32,1536]{3,2,1,0:T(8,128)(2,1)}, u32[]{:S(2)}) copy-start(bf16[4,8,32,1536]{3,2,1,0:T(8,128)(2,1)} %flip.1.gt_hbm) | copy-start | bytes 9437188
  20.6 19.7 %copy-start.1 = (bf16[2,768,512]{2,1,0:T(8,128)(2,1)S(1)}, bf16[2,768,512]{2,1,0:T(8,128)(2,1)}, u32[]{:S(2)}) copy-start(bf16[2,768,512]{2,1,0:T(8,128)(2,1)} %x_hbm.3) | copy-start | bytes 4718596
  24.3 18.7 %collective-permute-start = (f32[256,512]{1,0:T(8,128)S(1)}, f32[256,512]{1,0:T(8,128)S(1)}, u32[]{:S(2)}, u32[]{:S(2)}) collective-permute-start(f32[256,512]{1,0:T(8,128)S(1)} %get-tuple-element.8), channel_id=1, source_target_pairs={{80,160},{96,144},{112,128},{64,176},{144,96},{160,80},{176,64},{1... | collective-permute-start | bytes 1572872 | tf_op jit(solution)/shard_map/ppermute | solution.py:214
  35.9 12.3 %collective-permute-start.1 = (f32[256,512]{1,0:T(8,128)S(1)}, f32[256,512]{1,0:T(8,128)S(1)}, u32[]{:S(2)}, u32[]{:S(2)}) collective-permute-start(f32[256,512]{1,0:T(8,128)S(1)} %get-tuple-element.9), channel_id=1, source_target_pairs={{80,144},{96,160},{112,176},{64,128},{144,80},{160,96},{176,112},{... | collective-permute-start | bytes 1572872 | tf_op jit(solution)/shard_map/ppermute | solution.py:214
  37.8 12.3 %collective-permute-start.2 = (f32[256,512]{1,0:T(8,128)S(1)}, f32[256,512]{1,0:T(8,128)S(1)}, u32[]{:S(2)}, u32[]{:S(2)}) collective-permute-start(f32[256,512]{1,0:T(8,128)S(1)} %get-tuple-element.10), channel_id=1, source_target_pairs={{80,96},{96,80},{112,64},{64,112},{144,160},{160,144},{176,128},{1... | collective-permute-start | bytes 1572872 | tf_op jit(solution)/shard_map/ppermute | solution.py:214
